TPU v7x, 32 devices: a whole 2x2x4 slice. The times are simulated.
32 devices in a mesh: row: 8 (over y, x, core), col: 4 (over z).
Axes of the slice: x: 2, y: 2, z: 4, core: 2. Of those that a mesh axis runs over, the one named last changes fastest.
Arguments:
- a_vals: float32 [128, 512, 128], P('row', 'col'), may hold values from -6 to 6
- a_code: int32 [128, 4], P('row', 'col'), may hold values from -1 to 63, as said below
- b_vals: float32 [96, 512, 128], P('row', 'col'), may hold values from -0.25 to 0.25
- b_code: int32 [96, 4], P('row', 'col'), may hold values from -1 to 255, as said below
- panels: int32 [4], replicated, may hold values from 0 to 3, as said below
Outputs:
- c_band: float32 [1024, 4096], P('row', 'col')
Inputs may be any that keep to these rules, and one draw needn't show every extreme that they name: `a_code`: used slots of each device come first and name distinct block columns; empty slots hold -1; every device uses half or more of its 16 slots and some device uses all of them. `b_code`: used slots of each device come first and name distinct blocks; empty slots hold -1; every device uses half or more of its 12 slots and some device uses all of them. `panels`: each panel number appears once.
All inputs are finite; a program needn't handle non-finite values.
Results may differ from a plain program's by a relative error of at most 0.0003.
Values sent between devices are 32-bit elements; how exact they have to be, the bound alone decides.
No kernel may reach another device: no remote copies, remote signals or barrier semaphores. Data moves between devices by JAX's collectives and lax.ppermute only.
A program may use at most 64 MiB of HBM per device.

v0:
```python
import functools

import jax
import jax.numpy as jnp
from jax import lax
from jax.experimental import pallas as pl
from jax.experimental.pallas import tpu as pltpu
from jax.sharding import PartitionSpec as P

KPB = 64
STEPS = 2
JB = 8
TAIL = 8
MIB = 2**20

SMEM = pl.BlockSpec(memory_space=pltpu.SMEM)
VMEM = pl.BlockSpec(memory_space=pltpu.VMEM)
ANY = pl.BlockSpec(memory_space=pl.ANY)


def rows_of(slot, blk):
    return pl.ds(pl.multiple_of(slot * blk, blk), blk)


def prepare_kernel(chunks, a_code, b_code, panels, a_rows, b_rows, which, *refs):
    pieces, b_own = refs[: len(chunks)], refs[len(chunks)]
    tails, sems = refs[len(chunks) + 1 :]
    blk = a_rows.shape[1]
    copies = [
        pltpu.make_async_copy(a_rows.at[pl.ds(f * blk, (e - f) * blk)], piece.at[pl.ds(0, (e - f) * blk)], sems.at[i])
        for i, ((f, e), piece) in enumerate(zip(chunks, pieces))
    ]
    copies.append(pltpu.make_async_copy(b_rows, b_own.at[pl.ds(0, b_rows.shape[0])], sems.at[len(chunks)]))
    for copy in copies:
        copy.start()
    tails[...] = jnp.zeros_like(tails)
    for i, (code, into) in enumerate(((a_code, pieces[0]), (b_code, b_own))):
        tails[i, 0:1, 0 : code.shape[1]] = code[...].astype(jnp.float32)
        last = into.shape[0] - TAIL
        copy = pltpu.make_async_copy(tails.at[i], into.at[pl.ds(last, TAIL)], sems.at[len(chunks) + 1 + i])
        copy.start()
        copies.append(copy)
    lo = jnp.minimum(panels[0], panels[1])
    hi = jnp.maximum(panels[0], panels[1])
    which[0] = jnp.where(lo == 0, 0, lo + 1) + hi - 1
    for copy in copies:
        copy.wait()


def prepare(chunks, a_code, b_code, panels, a_rows, b_rows):
    blk = a_rows.shape[1]
    sizes = [(e - f) * blk for f, e in chunks]
    sizes[0] += TAIL
    sizes.append(b_rows.shape[0] + TAIL)
    return pl.pallas_call(
        functools.partial(prepare_kernel, chunks),
        out_shape=[jax.ShapeDtypeStruct((1,), jnp.int32)] + [jax.ShapeDtypeStruct((x, blk), jnp.float32) for x in sizes],
        in_specs=[VMEM, VMEM, SMEM, ANY, ANY],
        out_specs=[SMEM] + [ANY] * len(sizes),
        scratch_shapes=[pltpu.VMEM((2, TAIL, blk), jnp.float32), pltpu.SemaphoreType.DMA((len(chunks) + 3,))],
        name="prepare",
    )(a_code.T, b_code.T, panels, a_rows, b_rows)


def split(x):
    high = x.astype(jnp.bfloat16)
    low = (x - high.astype(jnp.float32)).astype(jnp.bfloat16)
    return high, low


def dot(x, y):
    return jnp.dot(x, y, preferred_element_type=jnp.float32)


def add_products(count, column, a_buf, b_buf, sems, c_ref):
    blk = a_buf.shape[1]

    def one(m, carry):
        for which, buf in enumerate((a_buf, b_buf)):
            pltpu.make_async_copy(buf.at[m], buf.at[m], sems.at[which, m]).wait()
        a_high, a_low = split(a_buf[m])
        b_high, b_low = split(b_buf[m])
        prod = dot(a_high, b_high) + (dot(a_high, b_low) + dot(a_low, b_high))
        c_ref[:, rows_of(column(m), blk)] += prod
        return carry

    lax.fori_loop(0, count, one, 0)


def start_from(refs, source, rows, into, sem):
    for i, ref in enumerate(refs):

        @pl.when(source == i)
        def _():
            pltpu.make_async_copy(ref.at[rows], into, sem).start()


def early_kernel(chunks, n_a, slots, a_at, b_at, *refs):
    group, sb = slots
    parts = max(1, len(chunks) - 1)
    n_b = len(refs) - n_a * parts - 13
    a_refs = [refs[i * parts : (i + 1) * parts] for i in range(n_a)]
    b_refs = refs[n_a * parts : n_a * parts + n_b]
    late, c_ref, b_late, tails, ints, codes, table, plan, a_buf, b_buf, sems, late_sems, tail_sems = refs[n_a * parts + n_b :]
    sa = chunks[-1][1]
    last_first = chunks[-1][0]
    blk = a_buf.shape[1]
    k_rows = KPB // group
    sources = [[a_at(s)] + [b_at(s, g) for g in range(group)] for s in range(STEPS)]
    sources = [x for step in sources for x in step]

    for t, source in enumerate(sources):
        holders = b_refs if t % (1 + group) else [arrays[0] for arrays in a_refs]
        start_from(holders, source, pl.ds(holders[0].shape[0] - TAIL, TAIL), tails.at[t], tail_sems.at[t])
    for s in range(STEPS):
        for k in range(KPB):
            table[s, k] = jnp.int32(-1)
    c_ref[...] = jnp.zeros_like(c_ref)
    ints[...] = jnp.zeros_like(ints)
    for t in range(len(sources)):
        pltpu.make_async_copy(tails.at[t], tails.at[t], tail_sems.at[t]).wait()
        ints[t : t + 1, :] = tails[t, 0:1, :].astype(jnp.int32)
    copy = pltpu.make_async_copy(ints, codes, tail_sems.at[len(sources)])
    copy.start()
    copy.wait()

    counts = (jnp.int32(0), jnp.int32(0))
    for s in range(STEPS):
        row_a = s * (1 + group)
        for slot in range(sa):
            code = codes[row_a, slot]

            @pl.when(code >= 0)
            def _():
                table[s, code] = jnp.int32(slot)

        for g in range(group):

            def one(slot, counts):
                n_early, n_late = counts
                code = codes[row_a + 1 + g, slot]
                k = jnp.where(code >= 0, g * k_rows + code // JB, 0)
                a_slot = table[s, k]
                ok = (code >= 0) & (a_slot >= 0)
                is_late = a_slot >= last_first

                @pl.when(ok & jnp.logical_not(is_late))
                def _():
                    plan[n_early] = code % JB
                    for i, arrays in enumerate(a_refs):

                        @pl.when(sources[row_a] == i)
                        def _():
                            for (f, e), ref in zip(chunks[:-1], arrays):

                                @pl.when((a_slot >= f) & (a_slot < e))
                                def _():
                                    rows = rows_of(a_slot - f, blk)
                                    pltpu.make_async_copy(ref.at[rows], a_buf.at[n_early], sems.at[0, n_early]).start()

                    start_from(b_refs, sources[row_a + 1 + g], rows_of(slot, blk), b_buf.at[n_early], sems.at[1, n_early])

                @pl.when(ok & is_late)
                def _():
                    late[1 + 3 * n_late] = sources[row_a]
                    late[2 + 3 * n_late] = a_slot - last_first
                    late[3 + 3 * n_late] = code % JB
                    into = b_late.at[rows_of(n_late, blk)]
                    start_from(b_refs, sources[row_a + 1 + g], rows_of(slot, blk), into, late_sems.at[n_late])

                is_late = is_late.astype(jnp.int32)
                ok = ok.astype(jnp.int32)
                return n_early + ok * (1 - is_late), n_late + ok * is_late

            counts = lax.fori_loop(0, sb, one, counts)
    late[0] = counts[1]
    add_products(counts[0], lambda m: plan[m], a_buf, b_buf, sems, c_ref)

    def wait(m, carry):
        into = b_late.at[rows_of(m, blk)]
        pltpu.make_async_copy(into, into, late_sems.at[m]).wait()
        return carry

    lax.fori_loop(0, counts[1], wait, 0)


def late_kernel(n_a, late, c_in, b_late, *refs):
    a_refs, (c_ref, a_buf, b_buf, sems) = refs[:n_a], refs[n_a:]
    blk = a_buf.shape[1]

    def fetch(m, carry):
        start_from(a_refs, late[1 + 3 * m], rows_of(late[2 + 3 * m], blk), a_buf.at[m], sems.at[0, m])
        pltpu.make_async_copy(b_late.at[rows_of(m, blk)], b_buf.at[m], sems.at[1, m]).start()
        return carry

    lax.fori_loop(0, late[0], fetch, 0)
    c_ref[...] = c_in[...]
    add_products(late[0], lambda m: late[3 + 3 * m], a_buf, b_buf, sems, c_ref)


def multiply(chunks, a_sources, b_sources, slots, a_at, b_at):
    group, sb = slots
    blk = b_sources[0].shape[1]
    most = STEPS * group * sb
    tails = STEPS * (1 + group)
    n_a = len(a_sources)
    first = chunks[:-1] or chunks
    buffers = [pltpu.VMEM((most, blk, blk), jnp.float32)] * 2 + [pltpu.SemaphoreType.DMA((2, most))]
    band = jax.ShapeDtypeStruct((blk, JB * blk), jnp.float32)
    late, c_early, b_late = pl.pallas_call(
        functools.partial(early_kernel, chunks, n_a, slots, a_at, b_at),
        out_shape=[
            jax.ShapeDtypeStruct((1 + 3 * most,), jnp.int32),
            band,
            jax.ShapeDtypeStruct((most * blk, blk), jnp.float32),
        ],
        in_specs=[ANY] * (n_a * len(first) + len(b_sources)),
        out_specs=[SMEM, VMEM, ANY],
        scratch_shapes=[
            pltpu.VMEM((tails, TAIL, blk), jnp.float32),
            pltpu.VMEM((TAIL, blk), jnp.int32),
            pltpu.SMEM((TAIL, blk), jnp.int32),
            pltpu.SMEM((STEPS, KPB), jnp.int32),
            pltpu.SMEM((most,), jnp.int32),
            *buffers,
            pltpu.SemaphoreType.DMA((most,)),
            pltpu.SemaphoreType.DMA((tails + 1,)),
        ],
        compiler_params=pltpu.CompilerParams(vmem_limit_bytes=24 * MIB),
        cost_estimate=pl.CostEstimate(flops=6 * 8 * blk**3, bytes_accessed=8 * MIB, transcendentals=0),
        name="early",
    )(*[x for arrays in a_sources for x in arrays[: len(first)]], *b_sources)
    return pl.pallas_call(
        functools.partial(late_kernel, n_a),
        out_shape=band,
        in_specs=[SMEM, VMEM, ANY] + [ANY] * n_a,
        out_specs=VMEM,
        scratch_shapes=buffers,
        compiler_params=pltpu.CompilerParams(vmem_limit_bytes=24 * MIB),
        cost_estimate=pl.CostEstimate(flops=6 * 2 * blk**3, bytes_accessed=2 * MIB, transcendentals=0),
        name="late",
    )(late, c_early, b_late, *[arrays[-1] for arrays in a_sources])


def as_rows(x):
    return x.reshape(-1, x.shape[-1])


def gathered(a_vals, a_code, b_vals, b_code, panels, group):
    chunks = [(0, a_vals.shape[0])]
    _, a_own, b_own = prepare(chunks, a_code, b_code, panels, as_rows(a_vals), as_rows(b_vals))
    a_all = lax.all_gather(a_own, "col")
    b_all = lax.all_gather(b_own, "row")
    a_sources, b_sources = [], []
    for step in range(STEPS):
        a_sources.append([lax.dynamic_index_in_dim(a_all, panels[step], 0, keepdims=False)])
        for g in range(group):
            b_sources.append(lax.dynamic_index_in_dim(b_all, panels[step] * group + g, 0, keepdims=False))
    slots = (group, b_vals.shape[0])
    return multiply(chunks, a_sources, b_sources, slots, lambda s: s, lambda s, g: s * group + g)


CHUNKS = [(0, 8), (8, 16)]
WINDOW = 5
UP = {
    (0, 1): [(None, ((0, 1), (1, 2)), {1: 0, 2: 1}), (0, ((1, 2), (2, 3)), {2: 0, 3: 1}), (1, ((2, 3),), {3: 0})],
    (0, 2): [(None, ((0, 1), (2, 3)), {1: 0, 3: 2}), (0, ((1, 2),), {2: 0}), (1, ((2, 3),), {3: 0})],
    (0, 3): [(None, ((0, 1),), {1: 0}), (0, ((1, 2),), {2: 0}), (1, ((2, 3),), {3: 0})],
    (1, 2): [(None, ((1, 2), (2, 3)), {2: 1, 3: 2}), (0, ((2, 3),), {3: 1})],
    (1, 3): [(None, ((1, 2),), {2: 1}), (0, ((2, 3),), {3: 1})],
    (2, 3): [(None, ((2, 3),), {3: 2})],
}


def chain_steps(roots, n):
    def flip(x):
        return n - 1 - x

    down = [
        (src, tuple((flip(x), flip(y)) for x, y in pairs), {flip(at): flip(p) for at, p in got.items()})
        for src, pairs, got in UP[tuple(sorted(map(flip, roots)))]
    ]
    return UP[roots], down


def pick(values, index):
    out = jnp.int32(values[0])
    for i, value in enumerate(values[1:], 1):
        out = jnp.where(index == i, jnp.int32(value), out)
    return out


def after(x, *earlier):
    return lax.optimization_barrier((x, *earlier))[0]


ORDER = {
    (0, 1): [
        "u0a", "x", "d0b", "u0b", "y", "u1a", "g", "so", "u1b", "u2a", "d0a", "sg", "sx", "u2b", "sy",
    ],
    (0, 2): [
        "u0a", "d0a", "x", "y", "d0b", "u0b", "u1a", "sx", "g", "u1b", "d1a", "u2a", "sy", "d1b", "u2b", "sg", "so",
    ],
    (0, 3): [
        "d0a", "u0a", "y", "x", "d0b", "u0b", "u1a", "d1a", "sy", "u1b", "g", "d1b", "u2a", "d2a", "sx", "u2b", "d2b",
        "so", "sg",
    ],
    (1, 2): [
        "u0b", "d0a", "y", "x", "so", "d0b", "u0a", "d1a", "sy", "g", "u1a", "u1b", "d1b", "sx", "sg",
    ],
}


def mirrored(name):
    return {"u": "d", "d": "u"}.get(name[0], name[0]) + name[1:]


def order_of(roots, n):
    if roots in ORDER:
        return ORDER[roots]
    return [mirrored(name) for name in ORDER[tuple(sorted(n - 1 - p for p in roots))]]


def pair_branch(roots, n, slots, pieces, b_own):
    group, _ = slots
    parts = "abcdefgh"[: len(pieces)]

    def exchange(bit):
        return "row", [(r, r ^ bit) for r in range(n * group)]

    moves = {"so": ("o", *exchange(1))}
    for q, name in enumerate("xyg", 1):
        moves[name] = ("o", *exchange(q * group))
        moves["s" + name] = (name, *exchange(1))
    held = dict(zip(parts, pieces), o=b_own)
    a_names = [list(parts)]
    a_table = [[0] * n for _ in roots]
    for way, steps in zip("ud", chain_steps(roots, n)):
        for number, (src, pairs, got) in enumerate(steps):
            for at, p in got.items():
                a_table[roots.index(p)][at] = len(a_names)
            for part in parts:
                moves[f"{way}{number}{part}"] = (part if src is None else f"{way}{src}{part}", "col", pairs)
            a_names.append([f"{way}{number}{part}" for part in parts])

    order = order_of(roots, n)
    ended = 0
    for i, name in enumerate(order):
        source, axis, pairs = moves.pop(name)
        x = held[source]
        ended = max(ended, i + 1 - WINDOW, order.index(source) + 1 if source in order else 0)
        if ended:
            x = lax.optimization_barrier((x, *[held[e] for e in order[max(0, ended - WINDOW) : ended] if e != source]))[0]
        held[name] = lax.ppermute(x, axis, pairs)
    assert not moves

    a_sources = [[held[name] for name in names] for names in a_names]
    b_sources = [held[name] for name in ("o", "x", "y", "g", "so", "sx", "sy", "sg")]

    def a_at(s):
        return pick(a_table[s], lax.axis_index("col"))

    def b_at(s, g):
        row = lax.axis_index("row")
        return ((row >> 1) ^ roots[s]) + jnp.where((row & 1) == g, 0, n)

    return multiply(CHUNKS, a_sources, b_sources, slots, a_at, b_at)


def shards(a_vals, a_code, b_vals, b_code, panels):
    n = lax.axis_size("col")
    group = lax.axis_size("row") // n
    if group != 2 or n != 4:
        return gathered(a_vals, a_code, b_vals, b_code, panels, group)
    which, *pieces, b_own = prepare(CHUNKS, a_code, b_code, panels, as_rows(a_vals), as_rows(b_vals))
    slots = (group, b_vals.shape[0])
    branches = [functools.partial(pair_branch, pair, n, slots) for pair in sorted(UP)]
    return lax.switch(which[0], branches, pieces, b_own)


def solution(mesh):
    return jax.shard_map(
        shards,
        mesh=mesh,
        in_specs=(
            P("row", "col", None),
            P("row", "col"),
            P("row", "col", None),
            P("row", "col"),
            P(),
        ),
        out_specs=P("row", "col"),
        check_vma=False,
    )
```

profile of v0, /device:TPU:0, one launch (start us, length us, event | category | flops | bytes accessed | tf_op | source)
XLA Modules:
  0.0 78.5 jit_solution(13011590421770209570)
XLA Ops:
  0.0 2.8 %prepare.1 = (s32[1]{0:T(128)}, f32[1032,128]{1,0:T(8,128)S(1)}, f32[1024,128]{1,0:T(8,128)S(1)}, f32[1544,128]{1,0:T(8,128)S(1)}) custom-call(s32[1,16]{1,0:T(1,128)} %bitcast.7, s32[1,12]{1,0:T(1,128)} %bitcast.8, s32[4]{0:T(128)} %panels.1, f32[2048,128]{1,0:T(8,128)} %bitcast.5, f32[1536,128]{1,0:T(8,128)} %bitcast.6), custom_call_target="tpu_custom_call" | custom-call | tf_op jit(solution)/shard_map/prepare/pallas_call | solution.py:55
  3.5 74.3 %conditional.1 = (f32[128,1024]{1,0:T(8,128)S(1)}) conditional(s32[]{:T(128)} %bitcast.4, (f32[1032,128]{1,0:T(8,128)S(1)}, f32[1544,128]{1,0:T(8,128)S(1)}, f32[1024,128]{1,0:T(8,128)S(1)}) %tuple.89, (f32[1032,128]{1,0:T(8,128)S(1)}, f32[1544,128]{1,0:T(8,128)S(1)}, f32[1024,128]{1,0:T(8,128)S(1)}) %tuple.89, ...), branch_computations={%region_0.0_spmd, %region_1.0_spmd, %region_2.0_spmd, %region_3.0_... | conditional | flops 125829120 | bytes 57885440 | solution.py:378
  3.7 3.0 %collective-permute-start.54 = (f32[1544,128]{1,0:T(8,128)S(1)}, f32[1544,128]{1,0:T(8,128)S(1)}, u32[]{:S(2)}, u32[]{:S(2)}) collective-permute-start(f32[1544,128]{1,0:T(8,128)S(1)} %get-tuple-element.108.refs_5_), channel_id=1, source_target_pairs={{0,16},{4,20},{8,24},{12,28},{16,0},{20,4},{24,8},{28,12},{1,17},{... | collective-permute-start | bytes 2371592 | tf_op jit(solution)/shard_map/cond/branch_3_fun/ppermute | solution.py:354
  6.7 1.5 %collective-permute-start.55 = (f32[1544,128]{1,0:T(8,128)S(1)}, f32[1544,128]{1,0:T(8,128)S(1)}, u32[]{:S(2)}, u32[]{:S(2)}) collective-permute-start(f32[1544,128]{1,0:T(8,128)S(1)} %get-tuple-element.108.refs_5_), channel_id=1, source_target_pairs={{0,8},{4,12},{8,0},{12,4},{16,24},{20,28},{24,16},{28,20},{1,9},{5... | collective-permute-start | bytes 2371592 | tf_op jit(solution)/shard_map/cond/branch_3_fun/ppermute | solution.py:354
  8.2 0.0 collective-permute-start.56
  8.2 1.3 %collective-permute-start.52 = (f32[1032,128]{1,0:T(8,128)S(1)}, f32[1032,128]{1,0:T(8,128)S(1)}, u32[]{:S(2)}, u32[]{:S(2)}) collective-permute-start(f32[1032,128]{1,0:T(8,128)S(1)} %get-tuple-element.103.refs_0_), channel_id=1, source_target_pairs={{2,1},{1,0},{6,5},{5,4},{10,9},{9,8},{14,13},{13,12},{18,17},{17,1... | collective-permute-start | bytes 1585160 | tf_op jit(solution)/shard_map/cond/branch_3_fun/ppermute | solution.py:354
  9.5 0.7 collective-permute-start.51
  10.2 0.0 collective-permute-done.51.refs_1_
  10.2 14.3 %collective-permute-done.52.refs_3_ = f32[1032,128]{1,0:T(8,128)S(1)} collective-permute-done((f32[1032,128]{1,0:T(8,128)S(1)}, f32[1032,128]{1,0:T(8,128)S(1)}, u32[]{:S(2)}, u32[]{:S(2)}) %collective-permute-start.52) | collective-permute-done | bytes 528416 | tf_op jit(solution)/shard_map/cond/branch_3_fun/ppermute | solution.py:354
  24.5 0.0 collective-permute-done.54.refs_7_
  24.5 1.3 %collective-permute-done.55.refs_6_ = f32[1544,128]{1,0:T(8,128)S(1)} collective-permute-done((f32[1544,128]{1,0:T(8,128)S(1)}, f32[1544,128]{1,0:T(8,128)S(1)}, u32[]{:S(2)}, u32[]{:S(2)}) %collective-permute-start.55) | collective-permute-done | bytes 790560 | tf_op jit(solution)/shard_map/cond/branch_3_fun/ppermute | solution.py:354
  25.8 0.0 collective-permute-start.61
  25.8 0.0 collective-permute-done.56.refs_9_
  25.8 1.4 %collective-permute-start.60 = (f32[1544,128]{1,0:T(8,128)S(1)}, f32[1544,128]{1,0:T(8,128)S(1)}, u32[]{:S(2)}, u32[]{:S(2)}) collective-permute-start(f32[1544,128]{1,0:T(8,128)S(1)} %get-tuple-element.108.refs_5_), channel_id=1, source_target_pairs={{0,24},{4,28},{8,16},{12,20},{16,8},{20,12},{24,0},{28,4},{1,25},{... | collective-permute-start | bytes 2371592 | tf_op jit(solution)/shard_map/cond/branch_3_fun/ppermute | solution.py:354
  27.2 0.7 collective-permute-start.53
  27.9 1.3 %collective-permute-start.59 = (f32[1032,128]{1,0:T(8,128)S(1)}, f32[1032,128]{1,0:T(8,128)S(1)}, u32[]{:S(2)}, u32[]{:S(2)}) collective-permute-start(f32[1032,128]{1,0:T(8,128)S(1)} %collective-permute-done.52.refs_3_), channel_id=1, source_target_pairs={{1,0},{5,4},{9,8},{13,12},{17,16},{21,20},{25,24},{29,28}} | collective-permute-start | bytes 1585160 | tf_op jit(solution)/shard_map/cond/branch_3_fun/ppermute | solution.py:354
  29.2 1.3 %collective-permute-start.57 = (f32[1024,128]{1,0:T(8,128)S(1)}, f32[1024,128]{1,0:T(8,128)S(1)}, u32[]{:S(2)}, u32[]{:S(2)}) collective-permute-start(f32[1024,128]{1,0:T(8,128)S(1)} %get-tuple-element.105.refs_0_), channel_id=1, source_target_pairs={{2,1},{1,0},{6,5},{5,4},{10,9},{9,8},{14,13},{13,12},{18,17},{17,1... | collective-permute-start | bytes 1572872 | tf_op jit(solution)/shard_map/cond/branch_3_fun/ppermute | solution.py:354
  30.5 26.4 %collective-permute-done.57.refs_3_ = f32[1024,128]{1,0:T(8,128)S(1)} collective-permute-done((f32[1024,128]{1,0:T(8,128)S(1)}, f32[1024,128]{1,0:T(8,128)S(1)}, u32[]{:S(2)}, u32[]{:S(2)}) %collective-permute-start.57) | collective-permute-done | bytes 524320 | tf_op jit(solution)/shard_map/cond/branch_3_fun/ppermute | solution.py:354
  57.0 0.0 collective-permute-done.53.refs_1_
  57.0 0.0 collective-permute-done.59.refs_4_
  57.0 0.0 collective-permute-done.61.refs_11_
  57.0 0.1 collective-permute-start.62
  57.0 0.0 collective-permute-done.60.refs_8_
  57.1 0.5 collective-permute-start.63
  57.5 0.7 collective-permute-start.58
  58.2 0.7 collective-permute-start.64
  58.9 1.3 %collective-permute-start.65 = (f32[1024,128]{1,0:T(8,128)S(1)}, f32[1024,128]{1,0:T(8,128)S(1)}, u32[]{:S(2)}, u32[]{:S(2)}) collective-permute-start(f32[1024,128]{1,0:T(8,128)S(1)} %collective-permute-done.57.refs_3_), channel_id=1, source_target_pairs={{1,0},{5,4},{9,8},{13,12},{17,16},{21,20},{25,24},{29,28}} | collective-permute-start | bytes 1572872 | tf_op jit(solution)/shard_map/cond/branch_3_fun/ppermute | solution.py:354
  60.2 0.0 collective-permute-done.58.refs_2_
  60.3 0.0 collective-permute-done.62.refs_10_
  60.3 0.2 collective-permute-done.63.refs_12_
  60.5 8.1 %early.9 = (s32[145]{0:T(256)S(1)}, f32[128,1024]{1,0:T(8,128)S(1)}, f32[6144,128]{1,0:T(8,128)S(1)}) custom-call(f32[1032,128]{1,0:T(8,128)S(1)} %get-tuple-element.103.refs_0_, f32[1032,128]{1,0:T(8,128)S(1)} %collective-permute-done.53.refs_1_, f32[1032,128]{1,0:T(8,128)S(1)} %collective-permute-done.58.refs_2_, ...), custom_call_target="tpu_custom_call" | custom-call | flops 100663296 | bytes 8388608 | tf_op jit(solution)/shard_map/cond/branch_3_fun/early/pallas_call | solution.py:210
  68.6 0.0 collective-permute-done.64.refs_2_
  68.6 6.1 %collective-permute-done.65.refs_4_ = f32[1024,128]{1,0:T(8,128)S(1)} collective-permute-done((f32[1024,128]{1,0:T(8,128)S(1)}, f32[1024,128]{1,0:T(8,128)S(1)}, u32[]{:S(2)}, u32[]{:S(2)}) %collective-permute-start.65) | collective-permute-done | bytes 524320 | tf_op jit(solution)/shard_map/cond/branch_3_fun/ppermute | solution.py:354
  74.8 3.0 %late.9 = f32[128,1024]{1,0:T(8,128)S(1)} custom-call(s32[145]{0:T(256)S(1)} %get-tuple-element.112.late, f32[128,1024]{1,0:T(8,128)S(1)} %get-tuple-element.113.c_in, f32[6144,128]{1,0:T(8,128)S(1)} %get-tuple-element.114.b_late, f32[1024,128]{1,0:T(8,128)S(1)} %get-tuple-element.105.refs_0_, f32[1024,128]{1,0:T(8,128)S(1)} %collective-permute-done.51.refs_1_, ...), custom_call_target="tpu_custom_call" | custom-call | flops 25165824 | bytes 2097152 | tf_op jit(solution)/shard_map/cond/branch_3_fun/late/pallas_call | solution.py:233
  77.7 0.0 copy-start
  77.7 0.8 copy-done
Async XLA Ops:
  3.7 20.8 %collective-permute-start.54 = (f32[1544,128]{1,0:T(8,128)S(1)}, f32[1544,128]{1,0:T(8,128)S(1)}, u32[]{:S(2)}, u32[]{:S(2)}) collective-permute-start(f32[1544,128]{1,0:T(8,128)S(1)} %get-tuple-element.108.refs_5_), channel_id=1, source_target_pairs={{0,16},{4,20},{8,24},{12,28},{16,0},{20,4},{24,8},{28,12},{1,17},{... | collective-permute-start | bytes 2371592 | tf_op jit(solution)/shard_map/cond/branch_3_fun/ppermute | solution.py:354
  6.7 19.1 %collective-permute-start.55 = (f32[1544,128]{1,0:T(8,128)S(1)}, f32[1544,128]{1,0:T(8,128)S(1)}, u32[]{:S(2)}, u32[]{:S(2)}) collective-permute-start(f32[1544,128]{1,0:T(8,128)S(1)} %get-tuple-element.108.refs_5_), channel_id=1, source_target_pairs={{0,8},{4,12},{8,0},{12,4},{16,24},{20,28},{24,16},{28,20},{1,9},{5... | collective-permute-start | bytes 2371592 | tf_op jit(solution)/shard_map/cond/branch_3_fun/ppermute | solution.py:354
  8.2 17.6 %collective-permute-start.56 = (f32[1544,128]{1,0:T(8,128)S(1)}, f32[1544,128]{1,0:T(8,128)S(1)}, u32[]{:S(2)}, u32[]{:S(2)}) collective-permute-start(f32[1544,128]{1,0:T(8,128)S(1)} %get-tuple-element.108.refs_5_), channel_id=1, source_target_pairs={{0,4},{4,0},{8,12},{12,8},{16,20},{20,16},{24,28},{28,24},{1,5},{5... | collective-permute-start | bytes 2371592 | tf_op jit(solution)/shard_map/cond/branch_3_fun/ppermute | solution.py:354
  8.2 16.3 %collective-permute-start.52 = (f32[1032,128]{1,0:T(8,128)S(1)}, f32[1032,128]{1,0:T(8,128)S(1)}, u32[]{:S(2)}, u32[]{:S(2)}) collective-permute-start(f32[1032,128]{1,0:T(8,128)S(1)} %get-tuple-element.103.refs_0_), channel_id=1, source_target_pairs={{2,1},{1,0},{6,5},{5,4},{10,9},{9,8},{14,13},{13,12},{18,17},{17,1... | collective-permute-start | bytes 1585160 | tf_op jit(solution)/shard_map/cond/branch_3_fun/ppermute | solution.py:354
  9.5 0.7 collective-permute-start.51
  25.8 31.2 %collective-permute-start.61 = (f32[1544,128]{1,0:T(8,128)S(1)}, f32[1544,128]{1,0:T(8,128)S(1)}, u32[]{:S(2)}, u32[]{:S(2)}) collective-permute-start(f32[1544,128]{1,0:T(8,128)S(1)} %collective-permute-done.54.refs_7_), channel_id=1, source_target_pairs={{0,4},{4,0},{8,12},{12,8},{16,20},{20,16},{24,28},{28,24},{1,5},{5... | collective-permute-start | bytes 2371592 | tf_op jit(solution)/shard_map/cond/branch_3_fun/ppermute | solution.py:354
  25.8 31.2 %collective-permute-start.60 = (f32[1544,128]{1,0:T(8,128)S(1)}, f32[1544,128]{1,0:T(8,128)S(1)}, u32[]{:S(2)}, u32[]{:S(2)}) collective-permute-start(f32[1544,128]{1,0:T(8,128)S(1)} %get-tuple-element.108.refs_5_), channel_id=1, source_target_pairs={{0,24},{4,28},{8,16},{12,20},{16,8},{20,12},{24,0},{28,4},{1,25},{... | collective-permute-start | bytes 2371592 | tf_op jit(solution)/shard_map/cond/branch_3_fun/ppermute | solution.py:354
  27.2 29.7 %collective-permute-start.53 = (f32[1032,128]{1,0:T(8,128)S(1)}, f32[1032,128]{1,0:T(8,128)S(1)}, u32[]{:S(2)}, u32[]{:S(2)}) collective-permute-start(f32[1032,128]{1,0:T(8,128)S(1)} %get-tuple-element.103.refs_0_), channel_id=1, source_target_pairs={{1,2},{2,3},{5,6},{6,7},{9,10},{10,11},{13,14},{14,15},{17,18},{18... | collective-permute-start | bytes 1585160 | tf_op jit(solution)/shard_map/cond/branch_3_fun/ppermute | solution.py:354
  27.9 29.0 %collective-permute-start.59 = (f32[1032,128]{1,0:T(8,128)S(1)}, f32[1032,128]{1,0:T(8,128)S(1)}, u32[]{:S(2)}, u32[]{:S(2)}) collective-permute-start(f32[1032,128]{1,0:T(8,128)S(1)} %collective-permute-done.52.refs_3_), channel_id=1, source_target_pairs={{1,0},{5,4},{9,8},{13,12},{17,16},{21,20},{25,24},{29,28}} | collective-permute-start | bytes 1585160 | tf_op jit(solution)/shard_map/cond/branch_3_fun/ppermute | solution.py:354
  29.2 27.7 %collective-permute-start.57 = (f32[1024,128]{1,0:T(8,128)S(1)}, f32[1024,128]{1,0:T(8,128)S(1)}, u32[]{:S(2)}, u32[]{:S(2)}) collective-permute-start(f32[1024,128]{1,0:T(8,128)S(1)} %get-tuple-element.105.refs_0_), channel_id=1, source_target_pairs={{2,1},{1,0},{6,5},{5,4},{10,9},{9,8},{14,13},{13,12},{18,17},{17,1... | collective-permute-start | bytes 1572872 | tf_op jit(solution)/shard_map/cond/branch_3_fun/ppermute | solution.py:354
  57.0 3.3 %collective-permute-start.62 = (f32[1544,128]{1,0:T(8,128)S(1)}, f32[1544,128]{1,0:T(8,128)S(1)}, u32[]{:S(2)}, u32[]{:S(2)}) collective-permute-start(f32[1544,128]{1,0:T(8,128)S(1)} %collective-permute-done.55.refs_6_), channel_id=1, source_target_pairs={{0,4},{4,0},{8,12},{12,8},{16,20},{20,16},{24,28},{28,24},{1,5},{5... | collective-permute-start | bytes 2371592 | tf_op jit(solution)/shard_map/cond/branch_3_fun/ppermute | solution.py:354
  57.1 3.4 %collective-permute-start.63 = (f32[1544,128]{1,0:T(8,128)S(1)}, f32[1544,128]{1,0:T(8,128)S(1)}, u32[]{:S(2)}, u32[]{:S(2)}) collective-permute-start(f32[1544,128]{1,0:T(8,128)S(1)} %collective-permute-done.60.refs_8_), channel_id=1, source_target_pairs={{0,4},{4,0},{8,12},{12,8},{16,20},{20,16},{24,28},{28,24},{1,5},{5... | collective-permute-start | bytes 2371592 | tf_op jit(solution)/shard_map/cond/branch_3_fun/ppermute | solution.py:354
  57.5 2.7 %collective-permute-start.58 = (f32[1032,128]{1,0:T(8,128)S(1)}, f32[1032,128]{1,0:T(8,128)S(1)}, u32[]{:S(2)}, u32[]{:S(2)}) collective-permute-start(f32[1032,128]{1,0:T(8,128)S(1)} %collective-permute-done.53.refs_1_), channel_id=1, source_target_pairs={{2,3},{6,7},{10,11},{14,15},{18,19},{22,23},{26,27},{30,31}} | collective-permute-start | bytes 1585160 | tf_op jit(solution)/shard_map/cond/branch_3_fun/ppermute | solution.py:354
  58.2 10.4 %collective-permute-start.64 = (f32[1024,128]{1,0:T(8,128)S(1)}, f32[1024,128]{1,0:T(8,128)S(1)}, u32[]{:S(2)}, u32[]{:S(2)}) collective-permute-start(f32[1024,128]{1,0:T(8,128)S(1)} %collective-permute-done.51.refs_1_), channel_id=1, source_target_pairs={{2,3},{6,7},{10,11},{14,15},{18,19},{22,23},{26,27},{30,31}} | collective-permute-start | bytes 1572872 | tf_op jit(solution)/shard_map/cond/branch_3_fun/ppermute | solution.py:354
  58.9 15.8 %collective-permute-start.65 = (f32[1024,128]{1,0:T(8,128)S(1)}, f32[1024,128]{1,0:T(8,128)S(1)}, u32[]{:S(2)}, u32[]{:S(2)}) collective-permute-start(f32[1024,128]{1,0:T(8,128)S(1)} %collective-permute-done.57.refs_3_), channel_id=1, source_target_pairs={{1,0},{5,4},{9,8},{13,12},{17,16},{21,20},{25,24},{29,28}} | collective-permute-start | bytes 1572872 | tf_op jit(solution)/shard_map/cond/branch_3_fun/ppermute | solution.py:354
  77.7 0.8 %copy-start = (f32[128,1024]{1,0:T(8,128)}, f32[128,1024]{1,0:T(8,128)S(1)}, u32[]{:S(2)}) copy-start(f32[128,1024]{1,0:T(8,128)S(1)} %get-tuple-element.361) | copy-start | bytes 1572868
where the time goes:
time: 77.6 us; the launch traced here: 78.5 us
  waiting for transfers between devices  48.4 us (62%)
  starting transfers between devices  14.4 us (19%)
  Pallas kernels  13.9 us (18%)
  local copies, waits for them, and re-layouts  0.79 us (1%)
    ppermute x15, waiting for transfers between devices, pair_branch(): held[name] = lax.ppermute(x, axis, pairs)  48.4 us
    ppermute x15, starting transfers between devices, pair_branch(): held[name] = lax.ppermute(x, axis, pairs)  14.4 us
    pallas_call x1, Pallas kernels, multiply(): pl.pallas_call(functools.partial(early_kernel, chunks, n_a, slots, a_at,...  8.15 us
    pallas_call x1, Pallas kernels, multiply(): pl.pallas_call(functools.partial(late_kernel, n_a), out_shape=band, in_sp...  2.96 us
    pallas_call x1, Pallas kernels, prepare(): pl.pallas_call(functools.partial(prepare_kernel, chunks), out_shape=[jax....  2.81 us
  transfers between devices with their start and end apart: 15, of which 5 were waited for; matrix products, arithmetic and copies ran while one was open for 0% of the time, Pallas kernels for 10%

commit v1 on v0

--- a/solution.py
+++ b/solution.py
@@ -1,4 +1,5 @@
 import functools
+import itertools
 
 import jax
 import jax.numpy as jnp
@@ -261,26 +262,40 @@
 
 
 CHUNKS = [(0, 8), (8, 16)]
-WINDOW = 5
-UP = {
-    (0, 1): [(None, ((0, 1), (1, 2)), {1: 0, 2: 1}), (0, ((1, 2), (2, 3)), {2: 0, 3: 1}), (1, ((2, 3),), {3: 0})],
-    (0, 2): [(None, ((0, 1), (2, 3)), {1: 0, 3: 2}), (0, ((1, 2),), {2: 0}), (1, ((2, 3),), {3: 0})],
-    (0, 3): [(None, ((0, 1),), {1: 0}), (0, ((1, 2),), {2: 0}), (1, ((2, 3),), {3: 0})],
-    (1, 2): [(None, ((1, 2), (2, 3)), {2: 1, 3: 2}), (0, ((2, 3),), {3: 1})],
-    (1, 3): [(None, ((1, 2),), {2: 1}), (0, ((2, 3),), {3: 1})],
-    (2, 3): [(None, ((2, 3),), {3: 2})],
+ROUTES = {
+    (0, 1): [(None, ((0, 1), (1, 2))), (0, ((1, 2), (2, 3))), (1, ((2, 3), (3, 0)))],
+    (0, 2): [(None, ((0, 1), (2, 3))), (0, ((1, 2), (3, 1))), (1, ((1, 0), (2, 3)))],
+    (0, 3): [(None, ((0, 1), (3, 2))), (0, ((1, 2), (2, 1))), (1, ((2, 3), (1, 0)))],
+    (1, 2): [(None, ((1, 0), (2, 3))), (None, ((1, 2), (2, 1))), (1, ((1, 0), (2, 3)))],
 }
-
-
-def chain_steps(roots, n):
-    def flip(x):
-        return n - 1 - x
-
-    down = [
-        (src, tuple((flip(x), flip(y)) for x, y in pairs), {flip(at): flip(p) for at, p in got.items()})
-        for src, pairs, got in UP[tuple(sorted(map(flip, roots)))]
-    ]
-    return UP[roots], down
+WRITTEN = ("0a", "1a", "0b", "1b", "x", "y", "g", "2a", "2b", "sx", "sy", "so", "sg")
+WAITS = {
+    (0, 1): {
+        "sy": ("2a", "g", "sg"),
+    },
+    (0, 2): {
+        "1a": ("0a",), "sx": ("y", "x"), "2b": ("sx", "1b"), "sg": ("1b", "2a"),
+    },
+    (0, 3): {
+        "sx": ("y", "x"), "1b": ("x", "0b"), "2a": ("0b", "1a"), "sy": ("1a", "g"), "2b": ("sx", "1b"),
+        "sg": ("1b", "2a"), "so": ("1a",),
+    },
+    (1, 2): {
+        "0b": ("0a",), "2a": ("0a",), "2b": ("0b",), "sg": ("2a",), "so": ("1b",), "g": ("1a",),
+    },
+}
+
+
+def route_of(roots, n):
+    mirror = roots not in ROUTES
+    key = tuple(sorted(n - 1 - p for p in roots)) if mirror else roots
+    steps, brings = [], []
+    for source, pairs in ROUTES[key]:
+        if mirror:
+            pairs = tuple((n - 1 - x, n - 1 - y) for x, y in pairs)
+        steps.append((source, pairs))
+        brings.append({y: x if source is None else brings[source][x] for x, y in pairs})
+    return steps, brings, WAITS[key]
 
 
 def pick(values, index):
@@ -292,33 +307,6 @@
 
 def after(x, *earlier):
     return lax.optimization_barrier((x, *earlier))[0]
-
-
-ORDER = {
-    (0, 1): [
-        "u0a", "x", "d0b", "u0b", "y", "u1a", "g", "so", "u1b", "u2a", "d0a", "sg", "sx", "u2b", "sy",
-    ],
-    (0, 2): [
-        "u0a", "d0a", "x", "y", "d0b", "u0b", "u1a", "sx", "g", "u1b", "d1a", "u2a", "sy", "d1b", "u2b", "sg", "so",
-    ],
-    (0, 3): [
-        "d0a", "u0a", "y", "x", "d0b", "u0b", "u1a", "d1a", "sy", "u1b", "g", "d1b", "u2a", "d2a", "sx", "u2b", "d2b",
-        "so", "sg",
-    ],
-    (1, 2): [
-        "u0b", "d0a", "y", "x", "so", "d0b", "u0a", "d1a", "sy", "g", "u1a", "u1b", "d1b", "sx", "sg",
-    ],
-}
-
-
-def mirrored(name):
-    return {"u": "d", "d": "u"}.get(name[0], name[0]) + name[1:]
-
-
-def order_of(roots, n):
-    if roots in ORDER:
-        return ORDER[roots]
-    return [mirrored(name) for name in ORDER[tuple(sorted(n - 1 - p for p in roots))]]
 
 
 def pair_branch(roots, n, slots, pieces, b_own):
@@ -335,24 +323,23 @@
     held = dict(zip(parts, pieces), o=b_own)
     a_names = [list(parts)]
     a_table = [[0] * n for _ in roots]
-    for way, steps in zip("ud", chain_steps(roots, n)):
-        for number, (src, pairs, got) in enumerate(steps):
-            for at, p in got.items():
-                a_table[roots.index(p)][at] = len(a_names)
-            for part in parts:
-                moves[f"{way}{number}{part}"] = (part if src is None else f"{way}{src}{part}", "col", pairs)
-            a_names.append([f"{way}{number}{part}" for part in parts])
-
-    order = order_of(roots, n)
-    ended = 0
-    for i, name in enumerate(order):
-        source, axis, pairs = moves.pop(name)
-        x = held[source]
-        ended = max(ended, i + 1 - WINDOW, order.index(source) + 1 if source in order else 0)
-        if ended:
-            x = lax.optimization_barrier((x, *[held[e] for e in order[max(0, ended - WINDOW) : ended] if e != source]))[0]
-        held[name] = lax.ppermute(x, axis, pairs)
-    assert not moves
+    steps, brings, waits = route_of(roots, n)
+    for number, (source, pairs) in enumerate(steps):
+        for at, p in brings[number].items():
+            a_table[roots.index(p)][at] = len(a_names)
+        for part in parts:
+            moves[f"{number}{part}"] = (part if source is None else f"{source}{part}", "col", pairs)
+        a_names.append([f"{number}{part}" for part in parts])
+
+    while moves:
+        for name in [name for name in WRITTEN if name in moves]:
+            source, axis, pairs = moves[name]
+            if all(e in held for e in (source, *waits.get(name, ()))):
+                x = held[source]
+                if name in waits:
+                    x = lax.optimization_barrier((x, *[held[e] for e in waits[name]]))[0]
+                held[name] = lax.ppermute(x, axis, pairs)
+                del moves[name]
 
     a_sources = [[held[name] for name in names] for names in a_names]
     b_sources = [held[name] for name in ("o", "x", "y", "g", "so", "sx", "sy", "sg")]
@@ -374,7 +361,7 @@
         return gathered(a_vals, a_code, b_vals, b_code, panels, group)
     which, *pieces, b_own = prepare(CHUNKS, a_code, b_code, panels, as_rows(a_vals), as_rows(b_vals))
     slots = (group, b_vals.shape[0])
-    branches = [functools.partial(pair_branch, pair, n, slots) for pair in sorted(UP)]
+    branches = [functools.partial(pair_branch, pair, n, slots) for pair in itertools.combinations(range(n), 2)]
     return lax.switch(which[0], branches, pieces, b_own)
 
 

time: 77.6 us -> 78 us (level); the launches traced: 78.5 us -> 76.9 us
  Pallas kernels: 13.9 us -> 10.2 us
  waiting for transfers between devices: 48.4 us -> 52 us
  starting transfers between devices: 14.4 us -> 12.7 us
    ppermute x15 -> x13, waiting for transfers between devices: 48.4 us -> 52 us  [pair_branch(): held[name] = lax.ppermute(x, axis, pairs)]
    pallas_call x1, Pallas kernels: 8.15 us -> 5.92 us  [multiply(): pl.pallas_call(functools.partial(early_kernel, chunks, n_a, slots, a_at,...]
    ppermute x15 -> x13, starting transfers between devices: 14.4 us -> 12.7 us  [pair_branch(): held[name] = lax.ppermute(x, axis, pairs)]
    pallas_call x1, Pallas kernels: 2.96 us -> 1.45 us  [multiply(): pl.pallas_call(functools.partial(late_kernel, n_a), out_shape=band, in_sp...]
  transfers between devices with their start and end apart: 15 -> 13, of which waited for: 5 -> 7; matrix products, arithmetic and copies ran while one was open for 0% -> 0% of each run, Pallas kernels for 10% -> 8%
where the time goes in v1:
time: 78 us; the launch traced here: 76.9 us
  waiting for transfers between devices  52 us (67%)
  starting transfers between devices  12.7 us (16%)
  Pallas kernels  10.2 us (13%)
  local copies, waits for them, and re-layouts  0.79 us (1%)
    ppermute x13, waiting for transfers between devices, pair_branch(): held[name] = lax.ppermute(x, axis, pairs)  52 us
    ppermute x13, starting transfers between devices, pair_branch(): held[name] = lax.ppermute(x, axis, pairs)  12.7 us
    pallas_call x1, Pallas kernels, multiply(): pl.pallas_call(functools.partial(early_kernel, chunks, n_a, slots, a_at,...  5.92 us
    pallas_call x1, Pallas kernels, prepare(): pl.pallas_call(functools.partial(prepare_kernel, chunks), out_shape=[jax....  2.81 us
  transfers between devices with their start and end apart: 13, of which 7 were waited for; matrix products, arithmetic and copies ran while one was open for 0% of the time, Pallas kernels for 8%

profile of v1, /device:TPU:0, one launch (start us, length us, event | category | flops | bytes accessed | tf_op | source)
XLA Modules:
  0.0 76.9 jit_solution(17772489216401970747)
XLA Ops:
  0.0 2.8 %prepare.1 = (s32[1]{0:T(128)}, f32[1032,128]{1,0:T(8,128)S(1)}, f32[1024,128]{1,0:T(8,128)S(1)}, f32[1544,128]{1,0:T(8,128)S(1)}) custom-call(s32[1,16]{1,0:T(1,128)} %bitcast.7, s32[1,12]{1,0:T(1,128)} %bitcast.8, s32[4]{0:T(128)} %panels.1, f32[2048,128]{1,0:T(8,128)} %bitcast.5, f32[1536,128]{1,0:T(8,128)} %bitcast.6), custom_call_target="tpu_custom_call" | custom-call | tf_op jit(solution)/shard_map/prepare/pallas_call | solution.py:56
  3.5 72.6 %conditional.1 = (f32[128,1024]{1,0:T(8,128)S(1)}) conditional(s32[]{:T(128)} %bitcast.4, (f32[1032,128]{1,0:T(8,128)S(1)}, f32[1544,128]{1,0:T(8,128)S(1)}, f32[1024,128]{1,0:T(8,128)S(1)}) %tuple.46, (f32[1032,128]{1,0:T(8,128)S(1)}, f32[1544,128]{1,0:T(8,128)S(1)}, f32[1024,128]{1,0:T(8,128)S(1)}) %tuple.46, ...), branch_computations={%region_0.0_spmd, %region_1.0_spmd, %region_2.0_spmd, %region_3.0_... | conditional | flops 125829120 | bytes 45253136 | solution.py:365
  3.7 0.7 collective-permute-start.65
  4.4 4.0 %collective-permute-start.70 = (f32[1544,128]{1,0:T(8,128)S(1)}, f32[1544,128]{1,0:T(8,128)S(1)}, u32[]{:S(2)}, u32[]{:S(2)}) collective-permute-start(f32[1544,128]{1,0:T(8,128)S(1)} %get-tuple-element.101.refs_4_), channel_id=1, source_target_pairs={{0,24},{4,28},{8,16},{12,20},{16,8},{20,12},{24,0},{28,4},{1,25},{... | collective-permute-start | bytes 2371592 | tf_op jit(solution)/shard_map/cond/branch_5_fun/ppermute | solution.py:341
  8.4 0.0 collective-permute-done.65.refs_1_
  8.4 1.3 %collective-permute-start.66 = (f32[1032,128]{1,0:T(8,128)S(1)}, f32[1032,128]{1,0:T(8,128)S(1)}, u32[]{:S(2)}, u32[]{:S(2)}) collective-permute-start(f32[1032,128]{1,0:T(8,128)S(1)} %collective-permute-done.65.refs_1_), channel_id=1, source_target_pairs={{2,1},{1,0},{6,5},{5,4},{10,9},{9,8},{14,13},{13,12},{18,17},{17,1... | collective-permute-start | bytes 1585160 | tf_op jit(solution)/shard_map/cond/branch_5_fun/ppermute | solution.py:341
  9.6 0.6 collective-permute-start.69
  10.2 0.1 collective-permute-start.68
  10.3 16.5 %collective-permute-done.70.refs_7_ = f32[1544,128]{1,0:T(8,128)S(1)} collective-permute-done((f32[1544,128]{1,0:T(8,128)S(1)}, f32[1544,128]{1,0:T(8,128)S(1)}, u32[]{:S(2)}, u32[]{:S(2)}) %collective-permute-start.70) | collective-permute-done | bytes 790560 | tf_op jit(solution)/shard_map/cond/branch_5_fun/ppermute | solution.py:341
  26.9 0.0 collective-permute-start.73
  26.9 0.7 collective-permute-start.75
  27.6 7.8 %collective-permute-done.66.refs_2_ = f32[1032,128]{1,0:T(8,128)S(1)} collective-permute-done((f32[1032,128]{1,0:T(8,128)S(1)}, f32[1032,128]{1,0:T(8,128)S(1)}, u32[]{:S(2)}, u32[]{:S(2)}) %collective-permute-start.66) | collective-permute-done | bytes 528416 | tf_op jit(solution)/shard_map/cond/branch_5_fun/ppermute | solution.py:341
  35.4 1.9 %collective-permute-start.67 = (f32[1032,128]{1,0:T(8,128)S(1)}, f32[1032,128]{1,0:T(8,128)S(1)}, u32[]{:S(2)}, u32[]{:S(2)}) collective-permute-start(f32[1032,128]{1,0:T(8,128)S(1)} %collective-permute-done.66.refs_2_), channel_id=1, source_target_pairs={{1,0},{0,3},{5,4},{4,7},{9,8},{8,11},{13,12},{12,15},{17,16},{16,1... | collective-permute-start | bytes 1585160 | tf_op jit(solution)/shard_map/cond/branch_5_fun/ppermute | solution.py:341
  37.3 0.0 collective-permute-done.75.refs_1_
  37.3 1.3 %collective-permute-start.76 = (f32[1024,128]{1,0:T(8,128)S(1)}, f32[1024,128]{1,0:T(8,128)S(1)}, u32[]{:S(2)}, u32[]{:S(2)}) collective-permute-start(f32[1024,128]{1,0:T(8,128)S(1)} %collective-permute-done.75.refs_1_), channel_id=1, source_target_pairs={{2,1},{1,0},{6,5},{5,4},{10,9},{9,8},{14,13},{13,12},{18,17},{17,1... | collective-permute-start | bytes 1572872 | tf_op jit(solution)/shard_map/cond/branch_5_fun/ppermute | solution.py:341
  38.6 4.3 %collective-permute-done.69.refs_6_ = f32[1544,128]{1,0:T(8,128)S(1)} collective-permute-done((f32[1544,128]{1,0:T(8,128)S(1)}, f32[1544,128]{1,0:T(8,128)S(1)}, u32[]{:S(2)}, u32[]{:S(2)}) %collective-permute-start.69) | collective-permute-done | bytes 790560 | tf_op jit(solution)/shard_map/cond/branch_5_fun/ppermute | solution.py:341
  42.9 0.0 collective-permute-start.71
  42.9 0.3 collective-permute-done.68.refs_5_
  43.2 0.2 collective-permute-start.72
  43.4 0.0 collective-permute-done.73.refs_11_
  43.4 6.1 %collective-permute-done.67.refs_3_ = f32[1032,128]{1,0:T(8,128)S(1)} collective-permute-done((f32[1032,128]{1,0:T(8,128)S(1)}, f32[1032,128]{1,0:T(8,128)S(1)}, u32[]{:S(2)}, u32[]{:S(2)}) %collective-permute-start.67) | collective-permute-done | bytes 528416 | tf_op jit(solution)/shard_map/cond/branch_5_fun/ppermute | solution.py:341
  49.5 0.0 collective-permute-start.74
  49.5 11.3 %collective-permute-done.76.refs_2_ = f32[1024,128]{1,0:T(8,128)S(1)} collective-permute-done((f32[1024,128]{1,0:T(8,128)S(1)}, f32[1024,128]{1,0:T(8,128)S(1)}, u32[]{:S(2)}, u32[]{:S(2)}) %collective-permute-start.76) | collective-permute-done | bytes 524320 | tf_op jit(solution)/shard_map/cond/branch_5_fun/ppermute | solution.py:341
  60.8 1.9 %collective-permute-start.77 = (f32[1024,128]{1,0:T(8,128)S(1)}, f32[1024,128]{1,0:T(8,128)S(1)}, u32[]{:S(2)}, u32[]{:S(2)}) collective-permute-start(f32[1024,128]{1,0:T(8,128)S(1)} %collective-permute-done.76.refs_2_), channel_id=1, source_target_pairs={{1,0},{0,3},{5,4},{4,7},{9,8},{8,11},{13,12},{12,15},{17,16},{16,1... | collective-permute-start | bytes 1572872 | tf_op jit(solution)/shard_map/cond/branch_5_fun/ppermute | solution.py:341
  62.7 0.0 collective-permute-done.71.refs_8_
  62.8 0.0 collective-permute-done.72.refs_9_
  62.8 0.0 collective-permute-done.74.refs_10_
  62.8 5.9 %early.11 = (s32[145]{0:T(256)S(1)}, f32[128,1024]{1,0:T(8,128)S(1)}, f32[6144,128]{1,0:T(8,128)S(1)}) custom-call(f32[1032,128]{1,0:T(8,128)S(1)} %get-tuple-element.100.refs_0_, f32[1032,128]{1,0:T(8,128)S(1)} %collective-permute-done.65.refs_1_, f32[1032,128]{1,0:T(8,128)S(1)} %collective-permute-done.66.refs_2_, ...), custom_call_target="tpu_custom_call" | custom-call | flops 100663296 | bytes 8388608 | tf_op jit(solution)/shard_map/cond/branch_5_fun/early/pallas_call | solution.py:211
  68.7 5.7 %collective-permute-done.77.refs_3_ = f32[1024,128]{1,0:T(8,128)S(1)} collective-permute-done((f32[1024,128]{1,0:T(8,128)S(1)}, f32[1024,128]{1,0:T(8,128)S(1)}, u32[]{:S(2)}, u32[]{:S(2)}) %collective-permute-start.77) | collective-permute-done | bytes 524320 | tf_op jit(solution)/shard_map/cond/branch_5_fun/ppermute | solution.py:341
  74.4 1.5 %late.11 = f32[128,1024]{1,0:T(8,128)S(1)} custom-call(s32[145]{0:T(256)S(1)} %get-tuple-element.103.late, f32[128,1024]{1,0:T(8,128)S(1)} %get-tuple-element.104.c_in, f32[6144,128]{1,0:T(8,128)S(1)} %get-tuple-element.105.b_late, f32[1024,128]{1,0:T(8,128)S(1)} %get-tuple-element.106.refs_0_, f32[1024,128]{1,0:T(8,128)S(1)} %collective-permute-done.75.refs_1_, ...), custom_call_target="tpu_custom_call" | custom-call | flops 25165824 | bytes 2097152 | tf_op jit(solution)/shard_map/cond/branch_5_fun/late/pallas_call | solution.py:234
  76.1 0.0 copy-start
  76.1 0.8 %copy-done = f32[128,1024]{1,0:T(8,128)} copy-done((f32[128,1024]{1,0:T(8,128)}, f32[128,1024]{1,0:T(8,128)S(1)}, u32[]{:S(2)}) %copy-start) | copy-done | bytes 524312
Async XLA Ops:
  3.7 4.7 %collective-permute-start.65 = (f32[1032,128]{1,0:T(8,128)S(1)}, f32[1032,128]{1,0:T(8,128)S(1)}, u32[]{:S(2)}, u32[]{:S(2)}) collective-permute-start(f32[1032,128]{1,0:T(8,128)S(1)} %get-tuple-element.100.refs_0_), channel_id=1, source_target_pairs={{3,2},{2,1},{7,6},{6,5},{11,10},{10,9},{15,14},{14,13},{19,18},{18... | collective-permute-start | bytes 1585160 | tf_op jit(solution)/shard_map/cond/branch_5_fun/ppermute | solution.py:341
  4.4 22.5 %collective-permute-start.70 = (f32[1544,128]{1,0:T(8,128)S(1)}, f32[1544,128]{1,0:T(8,128)S(1)}, u32[]{:S(2)}, u32[]{:S(2)}) collective-permute-start(f32[1544,128]{1,0:T(8,128)S(1)} %get-tuple-element.101.refs_4_), channel_id=1, source_target_pairs={{0,24},{4,28},{8,16},{12,20},{16,8},{20,12},{24,0},{28,4},{1,25},{... | collective-permute-start | bytes 2371592 | tf_op jit(solution)/shard_map/cond/branch_5_fun/ppermute | solution.py:341
  8.4 27.0 %collective-permute-start.66 = (f32[1032,128]{1,0:T(8,128)S(1)}, f32[1032,128]{1,0:T(8,128)S(1)}, u32[]{:S(2)}, u32[]{:S(2)}) collective-permute-start(f32[1032,128]{1,0:T(8,128)S(1)} %collective-permute-done.65.refs_1_), channel_id=1, source_target_pairs={{2,1},{1,0},{6,5},{5,4},{10,9},{9,8},{14,13},{13,12},{18,17},{17,1... | collective-permute-start | bytes 1585160 | tf_op jit(solution)/shard_map/cond/branch_5_fun/ppermute | solution.py:341
  9.6 33.3 %collective-permute-start.69 = (f32[1544,128]{1,0:T(8,128)S(1)}, f32[1544,128]{1,0:T(8,128)S(1)}, u32[]{:S(2)}, u32[]{:S(2)}) collective-permute-start(f32[1544,128]{1,0:T(8,128)S(1)} %get-tuple-element.101.refs_4_), channel_id=1, source_target_pairs={{0,16},{4,20},{8,24},{12,28},{16,0},{20,4},{24,8},{28,12},{1,17},{... | collective-permute-start | bytes 2371592 | tf_op jit(solution)/shard_map/cond/branch_5_fun/ppermute | solution.py:341
  10.2 33.0 %collective-permute-start.68 = (f32[1544,128]{1,0:T(8,128)S(1)}, f32[1544,128]{1,0:T(8,128)S(1)}, u32[]{:S(2)}, u32[]{:S(2)}) collective-permute-start(f32[1544,128]{1,0:T(8,128)S(1)} %get-tuple-element.101.refs_4_), channel_id=1, source_target_pairs={{0,8},{4,12},{8,0},{12,4},{16,24},{20,28},{24,16},{28,20},{1,9},{5... | collective-permute-start | bytes 2371592 | tf_op jit(solution)/shard_map/cond/branch_5_fun/ppermute | solution.py:341
  26.9 16.6 %collective-permute-start.73 = (f32[1544,128]{1,0:T(8,128)S(1)}, f32[1544,128]{1,0:T(8,128)S(1)}, u32[]{:S(2)}, u32[]{:S(2)}) collective-permute-start(f32[1544,128]{1,0:T(8,128)S(1)} %collective-permute-done.70.refs_7_), channel_id=1, source_target_pairs={{0,4},{4,0},{8,12},{12,8},{16,20},{20,16},{24,28},{28,24},{1,5},{5... | collective-permute-start | bytes 2371592 | tf_op jit(solution)/shard_map/cond/branch_5_fun/ppermute | solution.py:341
  26.9 10.5 %collective-permute-start.75 = (f32[1024,128]{1,0:T(8,128)S(1)}, f32[1024,128]{1,0:T(8,128)S(1)}, u32[]{:S(2)}, u32[]{:S(2)}) collective-permute-start(f32[1024,128]{1,0:T(8,128)S(1)} %get-tuple-element.106.refs_0_), channel_id=1, source_target_pairs={{3,2},{2,1},{7,6},{6,5},{11,10},{10,9},{15,14},{14,13},{19,18},{18... | collective-permute-start | bytes 1572872 | tf_op jit(solution)/shard_map/cond/branch_5_fun/ppermute | solution.py:341
  35.4 14.1 %collective-permute-start.67 = (f32[1032,128]{1,0:T(8,128)S(1)}, f32[1032,128]{1,0:T(8,128)S(1)}, u32[]{:S(2)}, u32[]{:S(2)}) collective-permute-start(f32[1032,128]{1,0:T(8,128)S(1)} %collective-permute-done.66.refs_2_), channel_id=1, source_target_pairs={{1,0},{0,3},{5,4},{4,7},{9,8},{8,11},{13,12},{12,15},{17,16},{16,1... | collective-permute-start | bytes 1585160 | tf_op jit(solution)/shard_map/cond/branch_5_fun/ppermute | solution.py:341
  37.3 23.5 %collective-permute-start.76 = (f32[1024,128]{1,0:T(8,128)S(1)}, f32[1024,128]{1,0:T(8,128)S(1)}, u32[]{:S(2)}, u32[]{:S(2)}) collective-permute-start(f32[1024,128]{1,0:T(8,128)S(1)} %collective-permute-done.75.refs_1_), channel_id=1, source_target_pairs={{2,1},{1,0},{6,5},{5,4},{10,9},{9,8},{14,13},{13,12},{18,17},{17,1... | collective-permute-start | bytes 1572872 | tf_op jit(solution)/shard_map/cond/branch_5_fun/ppermute | solution.py:341
  42.9 19.8 %collective-permute-start.71 = (f32[1544,128]{1,0:T(8,128)S(1)}, f32[1544,128]{1,0:T(8,128)S(1)}, u32[]{:S(2)}, u32[]{:S(2)}) collective-permute-start(f32[1544,128]{1,0:T(8,128)S(1)} %get-tuple-element.101.refs_4_), channel_id=1, source_target_pairs={{0,4},{4,0},{8,12},{12,8},{16,20},{20,16},{24,28},{28,24},{1,5},{5... | collective-permute-start | bytes 2371592 | tf_op jit(solution)/shard_map/cond/branch_5_fun/ppermute | solution.py:341
  43.2 19.5 %collective-permute-start.72 = (f32[1544,128]{1,0:T(8,128)S(1)}, f32[1544,128]{1,0:T(8,128)S(1)}, u32[]{:S(2)}, u32[]{:S(2)}) collective-permute-start(f32[1544,128]{1,0:T(8,128)S(1)} %collective-permute-done.68.refs_5_), channel_id=1, source_target_pairs={{0,4},{4,0},{8,12},{12,8},{16,20},{20,16},{24,28},{28,24},{1,5},{5... | collective-permute-start | bytes 2371592 | tf_op jit(solution)/shard_map/cond/branch_5_fun/ppermute | solution.py:341
  49.5 13.3 %collective-permute-start.74 = (f32[1544,128]{1,0:T(8,128)S(1)}, f32[1544,128]{1,0:T(8,128)S(1)}, u32[]{:S(2)}, u32[]{:S(2)}) collective-permute-start(f32[1544,128]{1,0:T(8,128)S(1)} %collective-permute-done.69.refs_6_), channel_id=1, source_target_pairs={{0,4},{4,0},{8,12},{12,8},{16,20},{20,16},{24,28},{28,24},{1,5},{5... | collective-permute-start | bytes 2371592 | tf_op jit(solution)/shard_map/cond/branch_5_fun/ppermute | solution.py:341
  60.8 13.6 %collective-permute-start.77 = (f32[1024,128]{1,0:T(8,128)S(1)}, f32[1024,128]{1,0:T(8,128)S(1)}, u32[]{:S(2)}, u32[]{:S(2)}) collective-permute-start(f32[1024,128]{1,0:T(8,128)S(1)} %collective-permute-done.76.refs_2_), channel_id=1, source_target_pairs={{1,0},{0,3},{5,4},{4,7},{9,8},{8,11},{13,12},{12,15},{17,16},{16,1... | collective-permute-start | bytes 1572872 | tf_op jit(solution)/shard_map/cond/branch_5_fun/ppermute | solution.py:341
  76.1 0.8 %copy-start = (f32[128,1024]{1,0:T(8,128)}, f32[128,1024]{1,0:T(8,128)S(1)}, u32[]{:S(2)}) copy-start(f32[128,1024]{1,0:T(8,128)S(1)} %get-tuple-element.278) | copy-start | bytes 1572868

commit v2 on v1

--- a/solution.py
+++ b/solution.py
@@ -69,8 +69,12 @@
     return high, low
 
 
-def dot(x, y):
-    return jnp.dot(x, y, preferred_element_type=jnp.float32)
+def product(a, b):
+    a_high, a_low = split(a)
+    b_high, b_low = split(b)
+    left = jnp.concatenate([a_high, a_high, a_low], axis=1)
+    right = jnp.concatenate([b_high, b_low, b_high], axis=0)
+    return jnp.dot(left, right, preferred_element_type=jnp.float32)
 
 
 def add_products(count, column, a_buf, b_buf, sems, c_ref):
@@ -79,10 +83,7 @@
     def one(m, carry):
         for which, buf in enumerate((a_buf, b_buf)):
             pltpu.make_async_copy(buf.at[m], buf.at[m], sems.at[which, m]).wait()
-        a_high, a_low = split(a_buf[m])
-        b_high, b_low = split(b_buf[m])
-        prod = dot(a_high, b_high) + (dot(a_high, b_low) + dot(a_low, b_high))
-        c_ref[:, rows_of(column(m), blk)] += prod
+        c_ref[:, rows_of(column(m), blk)] += product(a_buf[m], b_buf[m])
         return carry
 
     lax.fori_loop(0, count, one, 0)
@@ -99,58 +100,60 @@
 def early_kernel(chunks, n_a, slots, a_at, b_at, *refs):
     group, sb = slots
     parts = max(1, len(chunks) - 1)
-    n_b = len(refs) - n_a * parts - 13
+    n_b = len(refs) - n_a * parts - 12
     a_refs = [refs[i * parts : (i + 1) * parts] for i in range(n_a)]
     b_refs = refs[n_a * parts : n_a * parts + n_b]
-    late, c_ref, b_late, tails, ints, codes, table, plan, a_buf, b_buf, sems, late_sems, tail_sems = refs[n_a * parts + n_b :]
+    late, c_ref, b_late, tails, found, found_s, plan, a_buf, b_buf, sems, late_sems, tail_sems = refs[n_a * parts + n_b :]
     sa = chunks[-1][1]
     last_first = chunks[-1][0]
     blk = a_buf.shape[1]
     k_rows = KPB // group
     sources = [[a_at(s)] + [b_at(s, g) for g in range(group)] for s in range(STEPS)]
-    sources = [x for step in sources for x in step]
-
-    for t, source in enumerate(sources):
-        holders = b_refs if t % (1 + group) else [arrays[0] for arrays in a_refs]
-        start_from(holders, source, pl.ds(holders[0].shape[0] - TAIL, TAIL), tails.at[t], tail_sems.at[t])
+
+    def tail(s, i):
+        return s * (1 + group) + i
+
     for s in range(STEPS):
-        for k in range(KPB):
-            table[s, k] = jnp.int32(-1)
+        for i, source in enumerate(sources[s]):
+            holders = b_refs if i else [arrays[0] for arrays in a_refs]
+            rows = pl.ds(holders[0].shape[0] - TAIL, TAIL)
+            start_from(holders, source, rows, tails.at[tail(s, i)], tail_sems.at[tail(s, i)])
     c_ref[...] = jnp.zeros_like(c_ref)
-    ints[...] = jnp.zeros_like(ints)
-    for t in range(len(sources)):
-        pltpu.make_async_copy(tails.at[t], tails.at[t], tail_sems.at[t]).wait()
-        ints[t : t + 1, :] = tails[t, 0:1, :].astype(jnp.int32)
-    copy = pltpu.make_async_copy(ints, codes, tail_sems.at[len(sources)])
+    found[...] = jnp.full_like(found, -1)
+    for i in range(STEPS * (1 + group)):
+        pltpu.make_async_copy(tails.at[i], tails.at[i], tail_sems.at[i]).wait()
+
+    for s in range(STEPS):
+        a_codes = tails[tail(s, 0), 0:1, :].astype(jnp.int32)
+        for g in range(group):
+            b_codes = tails[tail(s, 1 + g), 0:1, :].astype(jnp.int32)
+            used = (b_codes >= 0) & (lax.broadcasted_iota(jnp.int32, b_codes.shape, 1) < sb)
+            k = jnp.where(used, g * k_rows + b_codes // JB, -2)
+            hit = jnp.full_like(k, -1)
+            for slot in range(sa):
+                hit = jnp.where(a_codes[:, slot : slot + 1] == k, slot, hit)
+            found[s * group + g : s * group + g + 1, :] = jnp.where(hit >= 0, hit * JB + b_codes % JB, -1)
+    copy = pltpu.make_async_copy(found, found_s, tail_sems.at[STEPS * (1 + group)])
     copy.start()
     copy.wait()
 
     counts = (jnp.int32(0), jnp.int32(0))
     for s in range(STEPS):
-        row_a = s * (1 + group)
-        for slot in range(sa):
-            code = codes[row_a, slot]
-
-            @pl.when(code >= 0)
-            def _():
-                table[s, code] = jnp.int32(slot)
-
         for g in range(group):
 
             def one(slot, counts):
                 n_early, n_late = counts
-                code = codes[row_a + 1 + g, slot]
-                k = jnp.where(code >= 0, g * k_rows + code // JB, 0)
-                a_slot = table[s, k]
-                ok = (code >= 0) & (a_slot >= 0)
+                hit = found_s[s * group + g, slot]
+                a_slot = hit // JB
+                early = (hit >= 0) & (a_slot < last_first)
                 is_late = a_slot >= last_first
 
-                @pl.when(ok & jnp.logical_not(is_late))
+                @pl.when(early)
                 def _():
-                    plan[n_early] = code % JB
+                    plan[n_early] = hit % JB
                     for i, arrays in enumerate(a_refs):
 
-                        @pl.when(sources[row_a] == i)
+                        @pl.when(sources[s][0] == i)
                         def _():
                             for (f, e), ref in zip(chunks[:-1], arrays):
 
@@ -159,19 +162,17 @@
                                     rows = rows_of(a_slot - f, blk)
                                     pltpu.make_async_copy(ref.at[rows], a_buf.at[n_early], sems.at[0, n_early]).start()
 
-                    start_from(b_refs, sources[row_a + 1 + g], rows_of(slot, blk), b_buf.at[n_early], sems.at[1, n_early])
-
-                @pl.when(ok & is_late)
+                    start_from(b_refs, sources[s][1 + g], rows_of(slot, blk), b_buf.at[n_early], sems.at[1, n_early])
+
+                @pl.when(is_late)
                 def _():
-                    late[1 + 3 * n_late] = sources[row_a]
+                    late[1 + 3 * n_late] = sources[s][0]
                     late[2 + 3 * n_late] = a_slot - last_first
-                    late[3 + 3 * n_late] = code % JB
+                    late[3 + 3 * n_late] = hit % JB
                     into = b_late.at[rows_of(n_late, blk)]
-                    start_from(b_refs, sources[row_a + 1 + g], rows_of(slot, blk), into, late_sems.at[n_late])
-
-                is_late = is_late.astype(jnp.int32)
-                ok = ok.astype(jnp.int32)
-                return n_early + ok * (1 - is_late), n_late + ok * is_late
+                    start_from(b_refs, sources[s][1 + g], rows_of(slot, blk), into, late_sems.at[n_late])
+
+                return n_early + early.astype(jnp.int32), n_late + is_late.astype(jnp.int32)
 
             counts = lax.fori_loop(0, sb, one, counts)
     late[0] = counts[1]
@@ -199,7 +200,7 @@
     add_products(late[0], lambda m: late[3 + 3 * m], a_buf, b_buf, sems, c_ref)
 
 
-def multiply(chunks, a_sources, b_sources, slots, a_at, b_at):
+def add_early(chunks, a_sources, b_sources, slots, a_at, b_at):
     group, sb = slots
     blk = b_sources[0].shape[1]
     most = STEPS * group * sb
@@ -219,9 +220,8 @@
         out_specs=[SMEM, VMEM, ANY],
         scratch_shapes=[
             pltpu.VMEM((tails, TAIL, blk), jnp.float32),
-            pltpu.VMEM((TAIL, blk), jnp.int32),
-            pltpu.SMEM((TAIL, blk), jnp.int32),
-            pltpu.SMEM((STEPS, KPB), jnp.int32),
+            pltpu.VMEM((max(8, STEPS * group), blk), jnp.int32),
+            pltpu.SMEM((max(8, STEPS * group), blk), jnp.int32),
             pltpu.SMEM((most,), jnp.int32),
             *buffers,
             pltpu.SemaphoreType.DMA((most,)),
@@ -231,16 +231,23 @@
         cost_estimate=pl.CostEstimate(flops=6 * 8 * blk**3, bytes_accessed=8 * MIB, transcendentals=0),
         name="early",
     )(*[x for arrays in a_sources for x in arrays[: len(first)]], *b_sources)
+    return late, c_early, b_late
+
+
+def add_late(late, c_early, b_late, a_last):
+    blk = a_last[0].shape[1]
+    most = (late.shape[0] - 1) // 3
+    buffers = [pltpu.VMEM((most, blk, blk), jnp.float32)] * 2 + [pltpu.SemaphoreType.DMA((2, most))]
     return pl.pallas_call(
-        functools.partial(late_kernel, n_a),
-        out_shape=band,
-        in_specs=[SMEM, VMEM, ANY] + [ANY] * n_a,
+        functools.partial(late_kernel, len(a_last)),
+        out_shape=jax.ShapeDtypeStruct(c_early.shape, c_early.dtype),
+        in_specs=[SMEM, VMEM, ANY] + [ANY] * len(a_last),
         out_specs=VMEM,
         scratch_shapes=buffers,
         compiler_params=pltpu.CompilerParams(vmem_limit_bytes=24 * MIB),
         cost_estimate=pl.CostEstimate(flops=6 * 2 * blk**3, bytes_accessed=2 * MIB, transcendentals=0),
         name="late",
-    )(late, c_early, b_late, *[arrays[-1] for arrays in a_sources])
+    )(late, c_early, b_late, *a_last)
 
 
 def as_rows(x):
@@ -258,7 +265,8 @@
         for g in range(group):
             b_sources.append(lax.dynamic_index_in_dim(b_all, panels[step] * group + g, 0, keepdims=False))
     slots = (group, b_vals.shape[0])
-    return multiply(chunks, a_sources, b_sources, slots, lambda s: s, lambda s, g: s * group + g)
+    early = add_early(chunks, a_sources, b_sources, slots, lambda s: s, lambda s, g: s * group + g)
+    return add_late(*early, [arrays[-1] for arrays in a_sources])
 
 
 CHUNKS = [(0, 8), (8, 16)]
@@ -274,7 +282,7 @@
         "sy": ("2a", "g", "sg"),
     },
     (0, 2): {
-        "1a": ("0a",), "sx": ("y", "x"), "2b": ("sx", "1b"), "sg": ("1b", "2a"),
+        "1a": ("0a",), "sx": ("y", "x"), "2b": ("sx", "1b"), "sg": ("1b", "2a", "g"), "sy": ("1b",),
     },
     (0, 3): {
         "sx": ("y", "x"), "1b": ("x", "0b"), "2a": ("0b", "1a"), "sy": ("1a", "g"), "2b": ("sx", "1b"),
@@ -351,7 +359,8 @@
         row = lax.axis_index("row")
         return ((row >> 1) ^ roots[s]) + jnp.where((row & 1) == g, 0, n)
 
-    return multiply(CHUNKS, a_sources, b_sources, slots, a_at, b_at)
+    early = add_early(CHUNKS, a_sources, b_sources, slots, a_at, b_at)
+    return early, [arrays[-1] for arrays in a_sources[1:]]
 
 
 def shards(a_vals, a_code, b_vals, b_code, panels):
@@ -362,7 +371,8 @@
     which, *pieces, b_own = prepare(CHUNKS, a_code, b_code, panels, as_rows(a_vals), as_rows(b_vals))
     slots = (group, b_vals.shape[0])
     branches = [functools.partial(pair_branch, pair, n, slots) for pair in itertools.combinations(range(n), 2)]
-    return lax.switch(which[0], branches, pieces, b_own)
+    early, a_last = lax.switch(which[0], branches, pieces, b_own)
+    return add_late(*early, [pieces[-1], *a_last])
 
 
 def solution(mesh):

time: 78 us -> 72.9 us (0.935)
  waiting for transfers between devices: 52 us -> 37.2 us
  starting transfers between devices: 12.7 us -> 20.8 us
  Pallas kernels: 10.2 us -> 13.4 us
  local copies, waits for them, and re-layouts: 0.79 us -> 0 us
    ppermute x13, waiting for transfers between devices: 52 us -> 37.2 us  [pair_branch(): held[name] = lax.ppermute(x, axis, pairs)]
    ppermute x13, starting transfers between devices: 12.7 us -> 20.8 us  [pair_branch(): held[name] = lax.ppermute(x, axis, pairs)]
    pallas_call x2, Pallas kernels: 7.37 us -> 10.6 us  [the longest x1 6.84 us: add_early(): pl.pallas_call(functools.partial(early_kernel, chunks, n_a, slots, a_at,...]
    unnamed x2 -> x0, local copies, waits for them, and re-layouts: 0.79 us -> none
  transfers between devices with their start and end apart: 13 -> 13, of which waited for: 7 -> 7; matrix products, arithmetic and copies ran while one was open for 0% -> 0% of each run, Pallas kernels for 8% -> 9%
where the time goes in v2:
time: 72.9 us; the launch traced here: 72.4 us
  waiting for transfers between devices  37.2 us (51%)
  starting transfers between devices  20.8 us (29%)
  Pallas kernels  13.4 us (18%)
  between operations  0.84 us (1%)
    ppermute x13, waiting for transfers between devices, pair_branch(): held[name] = lax.ppermute(x, axis, pairs)  37.2 us
    ppermute x13, starting transfers between devices, pair_branch(): held[name] = lax.ppermute(x, axis, pairs)  20.8 us
    pallas_call x1, Pallas kernels, add_early(): pl.pallas_call(functools.partial(early_kernel, chunks, n_a, slots, a_at,...  6.84 us
    pallas_call x1, Pallas kernels, add_late(): pl.pallas_call(functools.partial(late_kernel, len(a_last)), out_shape=jax...  3.78 us
    pallas_call x1, Pallas kernels, prepare(): pl.pallas_call(functools.partial(prepare_kernel, chunks), out_shape=[jax....  2.81 us
  transfers between devices with their start and end apart: 13, of which 7 were waited for; matrix products, arithmetic and copies ran while one was open for 0% of the time, Pallas kernels for 9%

profile of v2, /device:TPU:0, one launch (start us, length us, event | category | flops | bytes accessed | tf_op | source)
XLA Modules:
  0.0 72.4 jit_solution(13633859533433825755)
XLA Ops:
  0.0 2.8 %prepare.1 = (s32[1]{0:T(128)}, f32[1032,128]{1,0:T(8,128)S(1)}, f32[1024,128]{1,0:T(8,128)S(1)}, f32[1544,128]{1,0:T(8,128)S(1)}) custom-call(s32[1,16]{1,0:T(1,128)} %bitcast.7, s32[1,12]{1,0:T(1,128)} %bitcast.8, s32[4]{0:T(128)} %panels.1, f32[2048,128]{1,0:T(8,128)} %bitcast.5, f32[1536,128]{1,0:T(8,128)} %bitcast.6), custom_call_target="tpu_custom_call" | custom-call | tf_op jit(solution)/shard_map/prepare/pallas_call | solution.py:56
  3.5 64.9 %conditional.1 = (s32[145]{0:T(256)S(1)}, f32[128,1024]{1,0:T(8,128)S(1)}, f32[6144,128]{1,0:T(8,128)S(1)}, f32[1024,128]{1,0:T(8,128)}, f32[1024,128]{1,0:T(8,128)}, /*index=5*/f32[1024,128]{1,0:T(8,128)}) conditional(s32[]{:T(128)} %bitcast.4, (f32[1032,128]{1,0:T(8,128)S(1)}, f32[1544,128]{1,0:T(8,128)S(1)}, ...), branch_computations={%region_0.0_spmd, %region_1.0_spmd, %region_2.0_spmd, %region_3.0_... | conditional | flops 100663296 | bytes 43156024 | solution.py:374
  3.5 1.5 %collective-permute-start.52 = (f32[1032,128]{1,0:T(8,128)S(1)}, f32[1032,128]{1,0:T(8,128)S(1)}, u32[]{:S(2)}, u32[]{:S(2)}) collective-permute-start(f32[1032,128]{1,0:T(8,128)S(1)} %get-tuple-element.84.refs_0_), channel_id=1, source_target_pairs={{3,2},{1,0},{7,6},{5,4},{11,10},{9,8},{15,14},{13,12},{19,18},{17,... | collective-permute-start | bytes 1585160 | tf_op jit(solution)/shard_map/cond/branch_4_fun/ppermute | solution.py:349
  5.0 3.0 %collective-permute-start.56 = (f32[1544,128]{1,0:T(8,128)S(1)}, f32[1544,128]{1,0:T(8,128)S(1)}, u32[]{:S(2)}, u32[]{:S(2)}) collective-permute-start(f32[1544,128]{1,0:T(8,128)S(1)} %get-tuple-element.86.refs_4_), channel_id=1, source_target_pairs={{0,16},{4,20},{8,24},{12,28},{16,0},{20,4},{24,8},{28,12},{1,17},{... | collective-permute-start | bytes 2371592 | tf_op jit(solution)/shard_map/cond/branch_4_fun/ppermute | solution.py:349
  8.1 1.5 %collective-permute-start.55 = (f32[1544,128]{1,0:T(8,128)S(1)}, f32[1544,128]{1,0:T(8,128)S(1)}, u32[]{:S(2)}, u32[]{:S(2)}) collective-permute-start(f32[1544,128]{1,0:T(8,128)S(1)} %get-tuple-element.86.refs_4_), channel_id=1, source_target_pairs={{0,8},{4,12},{8,0},{12,4},{16,24},{20,28},{24,16},{28,20},{1,9},{5... | collective-permute-start | bytes 2371592 | tf_op jit(solution)/shard_map/cond/branch_4_fun/ppermute | solution.py:349
  9.6 10.3 %collective-permute-done.52.refs_1_ = f32[1032,128]{1,0:T(8,128)S(1)} collective-permute-done((f32[1032,128]{1,0:T(8,128)S(1)}, f32[1032,128]{1,0:T(8,128)S(1)}, u32[]{:S(2)}, u32[]{:S(2)}) %collective-permute-start.52) | collective-permute-done | bytes 528416 | tf_op jit(solution)/shard_map/cond/branch_4_fun/ppermute | solution.py:349
  19.8 5.3 %collective-permute-start.53 = (f32[1032,128]{1,0:T(8,128)S(1)}, f32[1032,128]{1,0:T(8,128)S(1)}, u32[]{:S(2)}, u32[]{:S(2)}) collective-permute-start(f32[1032,128]{1,0:T(8,128)S(1)} %collective-permute-done.52.refs_1_), channel_id=1, source_target_pairs={{2,1},{0,2},{6,5},{4,6},{10,9},{8,10},{14,13},{12,14},{18,17},{16,... | collective-permute-start | bytes 1585160 | tf_op jit(solution)/shard_map/cond/branch_4_fun/ppermute | solution.py:349
  25.1 1.3 %collective-permute-start.60 = (f32[1024,128]{1,0:T(8,128)S(1)}, f32[1024,128]{1,0:T(8,128)}, u32[]{:S(2)}, u32[]{:S(2)}) collective-permute-start(f32[1024,128]{1,0:T(8,128)S(1)} %get-tuple-element.88), channel_id=1, source_target_pairs={{3,2},{1,0},{7,6},{5,4},{11,10},{9,8},{15,14},{13,12},{19,18},{17,... | collective-permute-start | bytes 1572872 | tf_op jit(solution)/shard_map/cond/branch_4_fun/ppermute | solution.py:349
  26.4 2.5 %collective-permute-start.57 = (f32[1544,128]{1,0:T(8,128)S(1)}, f32[1544,128]{1,0:T(8,128)S(1)}, u32[]{:S(2)}, u32[]{:S(2)}) collective-permute-start(f32[1544,128]{1,0:T(8,128)S(1)} %get-tuple-element.86.refs_4_), channel_id=1, source_target_pairs={{0,24},{4,28},{8,16},{12,20},{16,8},{20,12},{24,0},{28,4},{1,25},{... | collective-permute-start | bytes 2371592 | tf_op jit(solution)/shard_map/cond/branch_4_fun/ppermute | solution.py:349
  28.9 6.5 %collective-permute-done.53.refs_2_ = f32[1032,128]{1,0:T(8,128)S(1)} collective-permute-done((f32[1032,128]{1,0:T(8,128)S(1)}, f32[1032,128]{1,0:T(8,128)S(1)}, u32[]{:S(2)}, u32[]{:S(2)}) %collective-permute-start.53) | collective-permute-done | bytes 528416 | tf_op jit(solution)/shard_map/cond/branch_4_fun/ppermute | solution.py:349
  35.5 1.3 %collective-permute-start.54 = (f32[1032,128]{1,0:T(8,128)S(1)}, f32[1032,128]{1,0:T(8,128)S(1)}, u32[]{:S(2)}, u32[]{:S(2)}) collective-permute-start(f32[1032,128]{1,0:T(8,128)S(1)} %collective-permute-done.53.refs_2_), channel_id=1, source_target_pairs={{2,3},{1,0},{6,7},{5,4},{10,11},{9,8},{14,15},{13,12},{18,19},{17,... | collective-permute-start | bytes 1585160 | tf_op jit(solution)/shard_map/cond/branch_4_fun/ppermute | solution.py:349
  36.8 4.4 %collective-permute-done.60 = f32[1024,128]{1,0:T(8,128)} collective-permute-done((f32[1024,128]{1,0:T(8,128)S(1)}, f32[1024,128]{1,0:T(8,128)}, u32[]{:S(2)}, u32[]{:S(2)}) %collective-permute-start.60) | collective-permute-done | bytes 524320 | tf_op jit(solution)/shard_map/cond/branch_4_fun/ppermute | solution.py:349
  41.1 2.1 %collective-permute-start.61 = (f32[1024,128]{1,0:T(8,128)}, f32[1024,128]{1,0:T(8,128)}, u32[]{:S(2)}, u32[]{:S(2)}) collective-permute-start(f32[1024,128]{1,0:T(8,128)} %collective-permute-done.60), channel_id=1, source_target_pairs={{2,1},{0,2},{6,5},{4,6},{10,9},{8,10},{14,13},{12,14},{18,17},{16,... | collective-permute-start | bytes 1572872 | tf_op jit(solution)/shard_map/cond/branch_4_fun/ppermute | solution.py:349
  43.2 0.0 collective-permute-done.56.refs_6_
  43.2 0.0 collective-permute-done.55.refs_5_
  43.2 0.0 collective-permute-start.59
  43.2 0.5 collective-permute-start.58
  43.7 8.1 %collective-permute-done.61 = f32[1024,128]{1,0:T(8,128)} collective-permute-done((f32[1024,128]{1,0:T(8,128)}, f32[1024,128]{1,0:T(8,128)}, u32[]{:S(2)}, u32[]{:S(2)}) %collective-permute-start.61) | collective-permute-done | bytes 524320 | tf_op jit(solution)/shard_map/cond/branch_4_fun/ppermute | solution.py:349
  51.8 0.0 collective-permute-start.62
  51.8 0.0 collective-permute-done.57.refs_7_
  51.8 0.0 collective-permute-done.54.refs_3_
  51.8 0.5 collective-permute-start.63
  52.3 0.0 collective-permute-done.59.refs_9_
  52.3 1.3 %collective-permute-start.64 = (f32[1024,128]{1,0:T(8,128)}, f32[1024,128]{1,0:T(8,128)}, u32[]{:S(2)}, u32[]{:S(2)}) collective-permute-start(f32[1024,128]{1,0:T(8,128)} %collective-permute-done.61), channel_id=1, source_target_pairs={{2,3},{1,0},{6,7},{5,4},{10,11},{9,8},{14,15},{13,12},{18,19},{17,... | collective-permute-start | bytes 1572872 | tf_op jit(solution)/shard_map/cond/branch_4_fun/ppermute | solution.py:349
  53.6 0.0 collective-permute-done.58.refs_8_
  53.6 0.5 collective-permute-done.62.refs_10_
  54.1 1.1 %collective-permute-done.63.refs_11_ = f32[1544,128]{1,0:T(8,128)S(1)} collective-permute-done((f32[1544,128]{1,0:T(8,128)S(1)}, f32[1544,128]{1,0:T(8,128)S(1)}, u32[]{:S(2)}, u32[]{:S(2)}) %collective-permute-start.63) | collective-permute-done | bytes 790560 | tf_op jit(solution)/shard_map/cond/branch_4_fun/ppermute | solution.py:349
  55.2 6.8 %early.10 = (s32[145]{0:T(256)S(1)}, f32[128,1024]{1,0:T(8,128)S(1)}, f32[6144,128]{1,0:T(8,128)S(1)}) custom-call(f32[1032,128]{1,0:T(8,128)S(1)} %get-tuple-element.84.refs_0_, f32[1032,128]{1,0:T(8,128)S(1)} %collective-permute-done.52.refs_1_, f32[1032,128]{1,0:T(8,128)S(1)} %collective-permute-done.53.refs_2_, ...), custom_call_target="tpu_custom_call" | custom-call | flops 100663296 | bytes 8388608 | tf_op jit(solution)/shard_map/cond/branch_4_fun/early/pallas_call | solution.py:212
  62.1 6.3 %collective-permute-done.64 = f32[1024,128]{1,0:T(8,128)} collective-permute-done((f32[1024,128]{1,0:T(8,128)}, f32[1024,128]{1,0:T(8,128)}, u32[]{:S(2)}, u32[]{:S(2)}) %collective-permute-start.64) | collective-permute-done | bytes 524320 | tf_op jit(solution)/shard_map/cond/branch_4_fun/ppermute | solution.py:349
  68.4 3.8 %late.1 = f32[128,1024]{1,0:T(8,128)} custom-call(s32[145]{0:T(256)S(1)} %get-tuple-element.116.late, f32[128,1024]{1,0:T(8,128)S(1)} %get-tuple-element.117.c_in, f32[6144,128]{1,0:T(8,128)S(1)} %get-tuple-element.118.b_late, f32[1024,128]{1,0:T(8,128)S(1)} %get-tuple-element.115.refs_0_, f32[1024,128]{1,0:T(8,128)} %get-tuple-element.119.refs_1_, ...), custom_call_target="tpu_custom_call" | custom-call | flops 25165824 | bytes 2097152 | tf_op jit(solution)/shard_map/late/pallas_call | solution.py:241
Async XLA Ops:
  3.5 16.3 %collective-permute-start.52 = (f32[1032,128]{1,0:T(8,128)S(1)}, f32[1032,128]{1,0:T(8,128)S(1)}, u32[]{:S(2)}, u32[]{:S(2)}) collective-permute-start(f32[1032,128]{1,0:T(8,128)S(1)} %get-tuple-element.84.refs_0_), channel_id=1, source_target_pairs={{3,2},{1,0},{7,6},{5,4},{11,10},{9,8},{15,14},{13,12},{19,18},{17,... | collective-permute-start | bytes 1585160 | tf_op jit(solution)/shard_map/cond/branch_4_fun/ppermute | solution.py:349
  5.0 38.2 %collective-permute-start.56 = (f32[1544,128]{1,0:T(8,128)S(1)}, f32[1544,128]{1,0:T(8,128)S(1)}, u32[]{:S(2)}, u32[]{:S(2)}) collective-permute-start(f32[1544,128]{1,0:T(8,128)S(1)} %get-tuple-element.86.refs_4_), channel_id=1, source_target_pairs={{0,16},{4,20},{8,24},{12,28},{16,0},{20,4},{24,8},{28,12},{1,17},{... | collective-permute-start | bytes 2371592 | tf_op jit(solution)/shard_map/cond/branch_4_fun/ppermute | solution.py:349
  8.1 35.2 %collective-permute-start.55 = (f32[1544,128]{1,0:T(8,128)S(1)}, f32[1544,128]{1,0:T(8,128)S(1)}, u32[]{:S(2)}, u32[]{:S(2)}) collective-permute-start(f32[1544,128]{1,0:T(8,128)S(1)} %get-tuple-element.86.refs_4_), channel_id=1, source_target_pairs={{0,8},{4,12},{8,0},{12,4},{16,24},{20,28},{24,16},{28,20},{1,9},{5... | collective-permute-start | bytes 2371592 | tf_op jit(solution)/shard_map/cond/branch_4_fun/ppermute | solution.py:349
  19.8 15.7 %collective-permute-start.53 = (f32[1032,128]{1,0:T(8,128)S(1)}, f32[1032,128]{1,0:T(8,128)S(1)}, u32[]{:S(2)}, u32[]{:S(2)}) collective-permute-start(f32[1032,128]{1,0:T(8,128)S(1)} %collective-permute-done.52.refs_1_), channel_id=1, source_target_pairs={{2,1},{0,2},{6,5},{4,6},{10,9},{8,10},{14,13},{12,14},{18,17},{16,... | collective-permute-start | bytes 1585160 | tf_op jit(solution)/shard_map/cond/branch_4_fun/ppermute | solution.py:349
  25.1 16.0 %collective-permute-start.60 = (f32[1024,128]{1,0:T(8,128)S(1)}, f32[1024,128]{1,0:T(8,128)}, u32[]{:S(2)}, u32[]{:S(2)}) collective-permute-start(f32[1024,128]{1,0:T(8,128)S(1)} %get-tuple-element.88), channel_id=1, source_target_pairs={{3,2},{1,0},{7,6},{5,4},{11,10},{9,8},{15,14},{13,12},{19,18},{17,... | collective-permute-start | bytes 1572872 | tf_op jit(solution)/shard_map/cond/branch_4_fun/ppermute | solution.py:349
  26.4 25.4 %collective-permute-start.57 = (f32[1544,128]{1,0:T(8,128)S(1)}, f32[1544,128]{1,0:T(8,128)S(1)}, u32[]{:S(2)}, u32[]{:S(2)}) collective-permute-start(f32[1544,128]{1,0:T(8,128)S(1)} %get-tuple-element.86.refs_4_), channel_id=1, source_target_pairs={{0,24},{4,28},{8,16},{12,20},{16,8},{20,12},{24,0},{28,4},{1,25},{... | collective-permute-start | bytes 2371592 | tf_op jit(solution)/shard_map/cond/branch_4_fun/ppermute | solution.py:349
  35.5 16.3 %collective-permute-start.54 = (f32[1032,128]{1,0:T(8,128)S(1)}, f32[1032,128]{1,0:T(8,128)S(1)}, u32[]{:S(2)}, u32[]{:S(2)}) collective-permute-start(f32[1032,128]{1,0:T(8,128)S(1)} %collective-permute-done.53.refs_2_), channel_id=1, source_target_pairs={{2,3},{1,0},{6,7},{5,4},{10,11},{9,8},{14,15},{13,12},{18,19},{17,... | collective-permute-start | bytes 1585160 | tf_op jit(solution)/shard_map/cond/branch_4_fun/ppermute | solution.py:349
  41.1 10.7 %collective-permute-start.61 = (f32[1024,128]{1,0:T(8,128)}, f32[1024,128]{1,0:T(8,128)}, u32[]{:S(2)}, u32[]{:S(2)}) collective-permute-start(f32[1024,128]{1,0:T(8,128)} %collective-permute-done.60), channel_id=1, source_target_pairs={{2,1},{0,2},{6,5},{4,6},{10,9},{8,10},{14,13},{12,14},{18,17},{16,... | collective-permute-start | bytes 1572872 | tf_op jit(solution)/shard_map/cond/branch_4_fun/ppermute | solution.py:349
  43.2 9.1 %collective-permute-start.59 = (f32[1544,128]{1,0:T(8,128)S(1)}, f32[1544,128]{1,0:T(8,128)S(1)}, u32[]{:S(2)}, u32[]{:S(2)}) collective-permute-start(f32[1544,128]{1,0:T(8,128)S(1)} %collective-permute-done.55.refs_5_), channel_id=1, source_target_pairs={{0,4},{4,0},{8,12},{12,8},{16,20},{20,16},{24,28},{28,24},{1,5},{5... | collective-permute-start | bytes 2371592 | tf_op jit(solution)/shard_map/cond/branch_4_fun/ppermute | solution.py:349
  43.2 10.4 %collective-permute-start.58 = (f32[1544,128]{1,0:T(8,128)S(1)}, f32[1544,128]{1,0:T(8,128)S(1)}, u32[]{:S(2)}, u32[]{:S(2)}) collective-permute-start(f32[1544,128]{1,0:T(8,128)S(1)} %get-tuple-element.86.refs_4_), channel_id=1, source_target_pairs={{0,4},{4,0},{8,12},{12,8},{16,20},{20,16},{24,28},{28,24},{1,5},{5... | collective-permute-start | bytes 2371592 | tf_op jit(solution)/shard_map/cond/branch_4_fun/ppermute | solution.py:349
  51.8 2.3 %collective-permute-start.62 = (f32[1544,128]{1,0:T(8,128)S(1)}, f32[1544,128]{1,0:T(8,128)S(1)}, u32[]{:S(2)}, u32[]{:S(2)}) collective-permute-start(f32[1544,128]{1,0:T(8,128)S(1)} %collective-permute-done.56.refs_6_), channel_id=1, source_target_pairs={{0,4},{4,0},{8,12},{12,8},{16,20},{20,16},{24,28},{28,24},{1,5},{5... | collective-permute-start | bytes 2371592 | tf_op jit(solution)/shard_map/cond/branch_4_fun/ppermute | solution.py:349
  51.8 3.4 %collective-permute-start.63 = (f32[1544,128]{1,0:T(8,128)S(1)}, f32[1544,128]{1,0:T(8,128)S(1)}, u32[]{:S(2)}, u32[]{:S(2)}) collective-permute-start(f32[1544,128]{1,0:T(8,128)S(1)} %collective-permute-done.57.refs_7_), channel_id=1, source_target_pairs={{0,4},{4,0},{8,12},{12,8},{16,20},{20,16},{24,28},{28,24},{1,5},{5... | collective-permute-start | bytes 2371592 | tf_op jit(solution)/shard_map/cond/branch_4_fun/ppermute | solution.py:349
  52.3 16.1 %collective-permute-start.64 = (f32[1024,128]{1,0:T(8,128)}, f32[1024,128]{1,0:T(8,128)}, u32[]{:S(2)}, u32[]{:S(2)}) collective-permute-start(f32[1024,128]{1,0:T(8,128)} %collective-permute-done.61), channel_id=1, source_target_pairs={{2,3},{1,0},{6,7},{5,4},{10,11},{9,8},{14,15},{13,12},{18,19},{17,... | collective-permute-start | bytes 1572872 | tf_op jit(solution)/shard_map/cond/branch_4_fun/ppermute | solution.py:349

commit v3 on v2

--- a/solution.py
+++ b/solution.py
@@ -97,12 +97,13 @@
             pltpu.make_async_copy(ref.at[rows], into, sem).start()
 
 
-def early_kernel(chunks, n_a, slots, a_at, b_at, *refs):
+def early_kernel(chunks, n_a, b_parts, slots, a_at, b_at, *refs):
     group, sb = slots
     parts = max(1, len(chunks) - 1)
-    n_b = len(refs) - n_a * parts - 12
+    n_b = sum(len(firsts) for firsts in b_parts)
     a_refs = [refs[i * parts : (i + 1) * parts] for i in range(n_a)]
-    b_refs = refs[n_a * parts : n_a * parts + n_b]
+    flat = iter(refs[n_a * parts : n_a * parts + n_b])
+    b_refs = [[(first, next(flat)) for first in firsts] for firsts in b_parts]
     late, c_ref, b_late, tails, found, found_s, plan, a_buf, b_buf, sems, late_sems, tail_sems = refs[n_a * parts + n_b :]
     sa = chunks[-1][1]
     last_first = chunks[-1][0]
@@ -115,9 +116,13 @@
 
     for s in range(STEPS):
         for i, source in enumerate(sources[s]):
-            holders = b_refs if i else [arrays[0] for arrays in a_refs]
-            rows = pl.ds(holders[0].shape[0] - TAIL, TAIL)
-            start_from(holders, source, rows, tails.at[tail(s, i)], tail_sems.at[tail(s, i)])
+            for j, holder in enumerate([held[-1][1] for held in b_refs] if i else [arrays[0] for arrays in a_refs]):
+
+                @pl.when(source == j)
+                def _():
+                    rows = pl.ds(holder.shape[0] - TAIL, TAIL)
+                    pltpu.make_async_copy(holder.at[rows], tails.at[tail(s, i)], tail_sems.at[tail(s, i)]).start()
+
     c_ref[...] = jnp.zeros_like(c_ref)
     found[...] = jnp.full_like(found, -1)
     for i in range(STEPS * (1 + group)):
@@ -137,6 +142,18 @@
     copy.start()
     copy.wait()
 
+    def start_b(source, slot, into, sem):
+        for i, held in enumerate(b_refs):
+
+            @pl.when(source == i)
+            def _():
+                for j, (first, ref) in enumerate(held):
+                    end = held[j + 1][0] if j + 1 < len(held) else sb
+
+                    @pl.when((slot >= first) & (slot < end))
+                    def _():
+                        pltpu.make_async_copy(ref.at[rows_of(slot - first, blk)], into, sem).start()
+
     counts = (jnp.int32(0), jnp.int32(0))
     for s in range(STEPS):
         for g in range(group):
@@ -162,7 +179,7 @@
                                     rows = rows_of(a_slot - f, blk)
                                     pltpu.make_async_copy(ref.at[rows], a_buf.at[n_early], sems.at[0, n_early]).start()
 
-                    start_from(b_refs, sources[s][1 + g], rows_of(slot, blk), b_buf.at[n_early], sems.at[1, n_early])
+                    start_b(sources[s][1 + g], slot, b_buf.at[n_early], sems.at[1, n_early])
 
                 @pl.when(is_late)
                 def _():
@@ -170,7 +187,7 @@
                     late[2 + 3 * n_late] = a_slot - last_first
                     late[3 + 3 * n_late] = hit % JB
                     into = b_late.at[rows_of(n_late, blk)]
-                    start_from(b_refs, sources[s][1 + g], rows_of(slot, blk), into, late_sems.at[n_late])
+                    start_b(sources[s][1 + g], slot, into, late_sems.at[n_late])
 
                 return n_early + early.astype(jnp.int32), n_late + is_late.astype(jnp.int32)
 
@@ -202,7 +219,8 @@
 
 def add_early(chunks, a_sources, b_sources, slots, a_at, b_at):
     group, sb = slots
-    blk = b_sources[0].shape[1]
+    b_flat = [array for held in b_sources for _, array in held]
+    blk = b_flat[0].shape[1]
     most = STEPS * group * sb
     tails = STEPS * (1 + group)
     n_a = len(a_sources)
@@ -210,13 +228,15 @@
     buffers = [pltpu.VMEM((most, blk, blk), jnp.float32)] * 2 + [pltpu.SemaphoreType.DMA((2, most))]
     band = jax.ShapeDtypeStruct((blk, JB * blk), jnp.float32)
     late, c_early, b_late = pl.pallas_call(
-        functools.partial(early_kernel, chunks, n_a, slots, a_at, b_at),
+        functools.partial(
+            early_kernel, chunks, n_a, [[first for first, _ in held] for held in b_sources], slots, a_at, b_at
+        ),
         out_shape=[
             jax.ShapeDtypeStruct((1 + 3 * most,), jnp.int32),
             band,
             jax.ShapeDtypeStruct((most * blk, blk), jnp.float32),
         ],
-        in_specs=[ANY] * (n_a * len(first) + len(b_sources)),
+        in_specs=[ANY] * (n_a * len(first) + len(b_flat)),
         out_specs=[SMEM, VMEM, ANY],
         scratch_shapes=[
             pltpu.VMEM((tails, TAIL, blk), jnp.float32),
@@ -230,7 +250,7 @@
         compiler_params=pltpu.CompilerParams(vmem_limit_bytes=24 * MIB),
         cost_estimate=pl.CostEstimate(flops=6 * 8 * blk**3, bytes_accessed=8 * MIB, transcendentals=0),
         name="early",
-    )(*[x for arrays in a_sources for x in arrays[: len(first)]], *b_sources)
+    )(*[x for arrays in a_sources for x in arrays[: len(first)]], *b_flat)
     return late, c_early, b_late
 
 
@@ -250,6 +270,30 @@
     )(late, c_early, b_late, *a_last)
 
 
+def collect_kernel(n, at, half, *refs):
+    sources, outs, sems = refs[:n], refs[n : n + 2 * STEPS], refs[n + 2 * STEPS]
+    rows = sources[0].shape[0]
+    for i, out in enumerate(outs):
+        part = pl.ds(half, rows - half) if i % 2 else pl.ds(0, half)
+        start_from(sources, at(i // 2), part, out, sems.at[i])
+    for i, out in enumerate(outs):
+        pltpu.make_async_copy(out, out, sems.at[i]).wait()
+
+
+def collect(sources, at, half):
+    rows, blk = sources[0].shape
+    sizes = [half, rows - half] * STEPS
+    return pl.pallas_call(
+        functools.partial(collect_kernel, len(sources), at, half),
+        out_shape=[jax.ShapeDtypeStruct((size, blk), sources[0].dtype) for size in sizes],
+        in_specs=[ANY] * len(sources),
+        out_specs=[ANY] * len(sizes),
+        scratch_shapes=[pltpu.SemaphoreType.DMA((len(sizes),))],
+        cost_estimate=pl.CostEstimate(flops=0, bytes_accessed=4 * MIB, transcendentals=0),
+        name="collect",
+    )(*sources)
+
+
 def as_rows(x):
     return x.reshape(-1, x.shape[-1])
 
@@ -263,7 +307,7 @@
     for step in range(STEPS):
         a_sources.append([lax.dynamic_index_in_dim(a_all, panels[step], 0, keepdims=False)])
         for g in range(group):
-            b_sources.append(lax.dynamic_index_in_dim(b_all, panels[step] * group + g, 0, keepdims=False))
+            b_sources.append([(0, lax.dynamic_index_in_dim(b_all, panels[step] * group + g, 0, keepdims=False))])
     slots = (group, b_vals.shape[0])
     early = add_early(chunks, a_sources, b_sources, slots, lambda s: s, lambda s, g: s * group + g)
     return add_late(*early, [arrays[-1] for arrays in a_sources])
@@ -276,21 +320,12 @@
     (0, 3): [(None, ((0, 1), (3, 2))), (0, ((1, 2), (2, 1))), (1, ((2, 3), (1, 0)))],
     (1, 2): [(None, ((1, 0), (2, 3))), (None, ((1, 2), (2, 1))), (1, ((1, 0), (2, 3)))],
 }
-WRITTEN = ("0a", "1a", "0b", "1b", "x", "y", "g", "2a", "2b", "sx", "sy", "so", "sg")
+WRITTEN = ("0a", "0b", "x", "y", "g", "1a", "1b", "2a", "2b", "s", "t", "u", "v")
 WAITS = {
-    (0, 1): {
-        "sy": ("2a", "g", "sg"),
-    },
-    (0, 2): {
-        "1a": ("0a",), "sx": ("y", "x"), "2b": ("sx", "1b"), "sg": ("1b", "2a", "g"), "sy": ("1b",),
-    },
-    (0, 3): {
-        "sx": ("y", "x"), "1b": ("x", "0b"), "2a": ("0b", "1a"), "sy": ("1a", "g"), "2b": ("sx", "1b"),
-        "sg": ("1b", "2a"), "so": ("1a",),
-    },
-    (1, 2): {
-        "0b": ("0a",), "2a": ("0a",), "2b": ("0b",), "sg": ("2a",), "so": ("1b",), "g": ("1a",),
-    },
+    (0, 1): {"g": ("x", "y"), "v": ("2a",)},
+    (0, 2): {"g": ("x", "y")},
+    (0, 3): {"g": ("x", "y")},
+    (1, 2): {"g": ("x", "y"), "2b": ("0b",), "2a": ("0a",)},
 }
 
 
@@ -318,16 +353,19 @@
 
 
 def pair_branch(roots, n, slots, pieces, b_own):
-    group, _ = slots
+    group, sb = slots
+    half = sb // 2
+    blk = b_own.shape[1]
     parts = "abcdefgh"[: len(pieces)]
 
     def exchange(bit):
         return "row", [(r, r ^ bit) for r in range(n * group)]
 
-    moves = {"so": ("o", *exchange(1))}
-    for q, name in enumerate("xyg", 1):
-        moves[name] = ("o", *exchange(q * group))
-        moves["s" + name] = (name, *exchange(1))
+    def from_chip(s):
+        return (lax.axis_index("row") >> 1) ^ roots[s]
+
+    moves = {name: ("o", *exchange(q * group)) for q, name in enumerate("xyg", 1)}
+    moves.update({name: ("own " + name, *exchange(1)) for name in "stuv"})
     held = dict(zip(parts, pieces), o=b_own)
     a_names = [list(parts)]
     a_table = [[0] * n for _ in roots]
@@ -342,6 +380,12 @@
     while moves:
         for name in [name for name in WRITTEN if name in moves]:
             source, axis, pairs = moves[name]
+            if name == "s" and source not in held and all(e in held for e in ("x", "y", "g", *waits.get("p", ()))):
+                last = held["g"]
+                if "p" in waits:
+                    last = lax.optimization_barrier((last, *[held[e] for e in waits["p"]]))[0]
+                halves = collect([held["o"], held["x"], held["y"], last], from_chip, half * blk)
+                held.update({"own " + name: x for name, x in zip("stuv", halves)})
             if all(e in held for e in (source, *waits.get(name, ()))):
                 x = held[source]
                 if name in waits:
@@ -350,14 +394,14 @@
                 del moves[name]
 
     a_sources = [[held[name] for name in names] for names in a_names]
-    b_sources = [held[name] for name in ("o", "x", "y", "g", "so", "sx", "sy", "sg")]
+    b_sources = [[(0, held[name])] for name in "oxyg"]
+    b_sources += [[(0, held[name]), (half, held[other])] for name, other in ("st", "uv")]
 
     def a_at(s):
         return pick(a_table[s], lax.axis_index("col"))
 
     def b_at(s, g):
-        row = lax.axis_index("row")
-        return ((row >> 1) ^ roots[s]) + jnp.where((row & 1) == g, 0, n)
+        return jnp.where((lax.axis_index("row") & 1) == g, from_chip(s), n + s)
 
     early = add_early(CHUNKS, a_sources, b_sources, slots, a_at, b_at)
     return early, [arrays[-1] for arrays in a_sources[1:]]

time: 72.9 us -> 154 us (2.11)
  the two profiles are of different devices: /device:TPU:0 before, /device:TPU:9 now
where the time goes in v3:
time: 154 us; the launch traced here: 155 us
  Pallas kernels  95.3 us (62%)
  waiting for transfers between devices  32.8 us (21%)
  starting transfers between devices  21.4 us (14%)
  local copies, waits for them, and re-layouts  4.33 us (3%)
    pallas_call x1, Pallas kernels, collect(): pl.pallas_call(functools.partial(collect_kernel, len(sources), at, half),...  49 us
    pallas_call x1, Pallas kernels, prepare(): pl.pallas_call(functools.partial(prepare_kernel, chunks), out_shape=[jax....  34.2 us
    ppermute x13, waiting for transfers between devices, pair_branch(): held[name] = lax.ppermute(x, axis, pairs)  32.8 us
    ppermute x13, starting transfers between devices, pair_branch(): held[name] = lax.ppermute(x, axis, pairs)  21.4 us
    pallas_call x1, Pallas kernels, add_early(): pl.pallas_call(functools.partial(early_kernel, chunks, n_a, [[first for f...  7.94 us
    cond x16, local copies, waits for them, and re-layouts  4.33 us
    pallas_call x1, Pallas kernels, add_late(): pl.pallas_call(functools.partial(late_kernel, len(a_last)), out_shape=jax...  4.13 us
  transfers between devices with their start and end apart: 13, of which 8 were waited for; matrix products, arithmetic and copies ran while one was open for 0% of the time, Pallas kernels for 37%

profile of v3, /device:TPU:9, one launch (start us, length us, event | category | flops | bytes accessed | tf_op | source)
XLA Modules:
  0.0 155.0 jit_solution(16619319810765094570)
XLA Ops:
  0.0 34.2 %prepare.1 = (s32[1]{0:T(128)}, f32[1032,128]{1,0:T(8,128)}, f32[1024,128]{1,0:T(8,128)}, f32[1544,128]{1,0:T(8,128)S(1)}) custom-call(s32[1,16]{1,0:T(1,128)} %bitcast.7, s32[1,12]{1,0:T(1,128)} %bitcast.8, s32[4]{0:T(128)} %panels.1, f32[2048,128]{1,0:T(8,128)} %bitcast.5, f32[1536,128]{1,0:T(8,128)} %bitcast.6), custom_call_target="tpu_custom_call" | custom-call | tf_op jit(solution)/shard_map/prepare/pallas_call | solution.py:56
  34.9 115.8 %conditional.1 = (s32[145]{0:T(256)S(1)}, f32[128,1024]{1,0:T(8,128)S(1)}, f32[6144,128]{1,0:T(8,128)S(1)}, f32[1024,128]{1,0:T(8,128)}, f32[1024,128]{1,0:T(8,128)}, /*index=5*/f32[1024,128]{1,0:T(8,128)}) conditional(s32[]{:T(128)} %bitcast.4, (f32[1032,128]{1,0:T(8,128)}, f32[1544,128]{1,0:T(8,128)S(1)}, ...), branch_computations={%region_0.0_spmd, %region_1.0_spmd, %region_2.0_spmd, %region_3.0_... | conditional | flops 100663296 | bytes 65258264 | solution.py:418
  34.9 0.0 copy-start.36
  34.9 3.2 %collective-permute-start = (f32[1032,128]{1,0:T(8,128)}, f32[1032,128]{1,0:T(8,128)S(1)}, u32[]{:S(2)}, u32[]{:S(2)}) collective-permute-start(f32[1032,128]{1,0:T(8,128)} %get-tuple-element.41.refs_0_), channel_id=1, source_target_pairs={{0,1},{1,2},{4,5},{5,6},{8,9},{9,10},{12,13},{13,14},{16,17},{17,1... | collective-permute-start | bytes 1585160 | tf_op jit(solution)/shard_map/cond/branch_0_fun/ppermute | solution.py:393
  38.1 1.3 collective-permute-start.3
  39.4 1.2 collective-permute-start.4
  40.6 1.9 %collective-permute-start.10 = (f32[1024,128]{1,0:T(8,128)}, f32[1024,128]{1,0:T(8,128)S(1)}, u32[]{:S(2)}, u32[]{:S(2)}) collective-permute-start(f32[1024,128]{1,0:T(8,128)} %get-tuple-element.52), channel_id=1, source_target_pairs={{0,1},{1,2},{4,5},{5,6},{8,9},{9,10},{12,13},{13,14},{16,17},{17,1... | collective-permute-start | bytes 1572872 | tf_op jit(solution)/shard_map/cond/branch_0_fun/ppermute | solution.py:393
  42.6 7.3 %collective-permute-done.refs_1_ = f32[1032,128]{1,0:T(8,128)S(1)} collective-permute-done((f32[1032,128]{1,0:T(8,128)}, f32[1032,128]{1,0:T(8,128)S(1)}, u32[]{:S(2)}, u32[]{:S(2)}) %collective-permute-start) | collective-permute-done | bytes 528416 | tf_op jit(solution)/shard_map/cond/branch_0_fun/ppermute | solution.py:393
  49.9 3.2 %collective-permute-start.1 = (f32[1032,128]{1,0:T(8,128)S(1)}, f32[1032,128]{1,0:T(8,128)S(1)}, u32[]{:S(2)}, u32[]{:S(2)}) collective-permute-start(f32[1032,128]{1,0:T(8,128)S(1)} %collective-permute-done.refs_1_), channel_id=1, source_target_pairs={{1,2},{2,3},{5,6},{6,7},{9,10},{10,11},{13,14},{14,15},{17,18},{18... | collective-permute-start | bytes 1585160 | tf_op jit(solution)/shard_map/cond/branch_0_fun/ppermute | solution.py:393
  53.1 3.2 %collective-permute-done.3.refs_1_.refs_5_ = f32[1544,128]{1,0:T(8,128)S(1)} collective-permute-done((f32[1544,128]{1,0:T(8,128)S(1)}, f32[1544,128]{1,0:T(8,128)S(1)}, u32[]{:S(2)}, u32[]{:S(2)}) %collective-permute-start.3) | collective-permute-done | bytes 790560 | tf_op jit(solution)/shard_map/cond/branch_0_fun/ppermute | solution.py:393
  56.4 0.0 copy-done.36
  56.4 0.0 copy-start.8
  56.4 0.9 collective-permute-done.4.refs_2_.refs_6_
  57.3 0.0 copy-start.20
  57.3 1.3 collective-permute-start.5
  58.6 2.5 %collective-permute-done.10 = f32[1024,128]{1,0:T(8,128)S(1)} collective-permute-done((f32[1024,128]{1,0:T(8,128)}, f32[1024,128]{1,0:T(8,128)S(1)}, u32[]{:S(2)}, u32[]{:S(2)}) %collective-permute-start.10) | collective-permute-done | bytes 524320 | tf_op jit(solution)/shard_map/cond/branch_0_fun/ppermute | solution.py:393
  61.1 0.0 copy-start.42
  61.1 4.0 %collective-permute-start.11 = (f32[1024,128]{1,0:T(8,128)S(1)}, f32[1024,128]{1,0:T(8,128)}, u32[]{:S(2)}, u32[]{:S(2)}) collective-permute-start(f32[1024,128]{1,0:T(8,128)S(1)} %collective-permute-done.10), channel_id=1, source_target_pairs={{1,2},{2,3},{5,6},{6,7},{9,10},{10,11},{13,14},{14,15},{17,18},{18... | collective-permute-start | bytes 1572872 | tf_op jit(solution)/shard_map/cond/branch_0_fun/ppermute | solution.py:393
  65.1 6.4 %collective-permute-done.1.refs_2_ = f32[1032,128]{1,0:T(8,128)S(1)} collective-permute-done((f32[1032,128]{1,0:T(8,128)S(1)}, f32[1032,128]{1,0:T(8,128)S(1)}, u32[]{:S(2)}, u32[]{:S(2)}) %collective-permute-start.1) | collective-permute-done | bytes 528416 | tf_op jit(solution)/shard_map/cond/branch_0_fun/ppermute | solution.py:393
  71.5 1.5 collective-permute-start.2
  73.0 9.8 %collective-permute-done.11 = f32[1024,128]{1,0:T(8,128)} collective-permute-done((f32[1024,128]{1,0:T(8,128)S(1)}, f32[1024,128]{1,0:T(8,128)}, u32[]{:S(2)}, u32[]{:S(2)}) %collective-permute-start.11) | collective-permute-done | bytes 524320 | tf_op jit(solution)/shard_map/cond/branch_0_fun/ppermute | solution.py:393
  82.8 0.0 copy-done.42
  82.8 1.5 collective-permute-start.12
  84.3 0.0 collective-permute-done.5.refs_3_.refs_7_
  84.3 0.0 copy-done.8
  84.3 0.0 copy-done.20
  84.3 0.0 copy-start.26
  84.3 0.9 copy-done.26
  85.2 49.0 %collect.6 = (f32[768,128]{1,0:T(8,128)}, f32[776,128]{1,0:T(8,128)}, f32[768,128]{1,0:T(8,128)}, f32[776,128]{1,0:T(8,128)}) custom-call(f32[1544,128]{1,0:T(8,128)} %copy-done.36, f32[1544,128]{1,0:T(8,128)} %copy-done.8, f32[1544,128]{1,0:T(8,128)} %copy-done.20, f32[1544,128]{1,0:T(8,128)} %copy-done.26), custom_call_target="tpu_custom_call" | custom-call | bytes 4194304 | tf_op jit(solution)/shard_map/cond/branch_0_fun/collect/pallas_call | solution.py:286
  134.2 1.6 %collective-permute-start.7 = (f32[776,128]{1,0:T(8,128)}, f32[776,128]{1,0:T(8,128)S(1)}, u32[]{:S(2)}, u32[]{:S(2)}) collective-permute-start(f32[776,128]{1,0:T(8,128)} %get-tuple-element.45), channel_id=1, source_target_pairs={{0,4},{4,0},{8,12},{12,8},{16,20},{20,16},{24,28},{28,24},{1,5},{5... | collective-permute-start | bytes 1191944 | tf_op jit(solution)/shard_map/cond/branch_0_fun/ppermute | solution.py:393
  135.9 0.0 collective-permute-done.2.refs_3_
  135.9 0.1 collective-permute-start.9
  135.9 0.4 collective-permute-start.6
  136.4 0.1 collective-permute-start.8
  136.5 2.1 %collective-permute-done.6.refs_8_ = f32[768,128]{1,0:T(8,128)S(1)} collective-permute-done((f32[768,128]{1,0:T(8,128)}, f32[768,128]{1,0:T(8,128)S(1)}, u32[]{:S(2)}, u32[]{:S(2)}) %collective-permute-start.6) | collective-permute-done | bytes 393248 | tf_op jit(solution)/shard_map/cond/branch_0_fun/ppermute | solution.py:393
  138.6 0.6 collective-permute-done.8.refs_10_
  139.1 0.0 collective-permute-done.7.refs_9_
  139.1 0.0 collective-permute-done.9.refs_11_
  139.1 0.0 copy-start.9
  139.1 1.1 copy-done.9
  140.3 0.0 copy-start.21
  140.3 1.1 copy-done.21
  141.4 0.0 copy-start.27
  141.4 1.1 copy-done.27
  142.5 7.9 %early.6 = (s32[145]{0:T(256)S(1)}, f32[128,1024]{1,0:T(8,128)S(1)}, f32[6144,128]{1,0:T(8,128)S(1)}) custom-call(f32[1032,128]{1,0:T(8,128)} %get-tuple-element.41.refs_0_, f32[1032,128]{1,0:T(8,128)S(1)} %collective-permute-done.refs_1_, f32[1032,128]{1,0:T(8,128)S(1)} %collective-permute-done.1.refs_2_, f32[1032,128]{1,0:T(8,128)} %collective-permute-done.2.refs_3_, ...), custom_call_target="tpu_custom_call" | custom-call | flops 100663296 | bytes 8388608 | tf_op jit(solution)/shard_map/cond/branch_0_fun/early/pallas_call | solution.py:230
  150.5 0.0 collective-permute-done.12
  150.7 4.1 %late.1 = f32[128,1024]{1,0:T(8,128)} custom-call(s32[145]{0:T(256)S(1)} %get-tuple-element.125.late, f32[128,1024]{1,0:T(8,128)S(1)} %get-tuple-element.126.c_in, f32[6144,128]{1,0:T(8,128)S(1)} %get-tuple-element.127.b_late, f32[1024,128]{1,0:T(8,128)} %get-tuple-element.124.refs_0_, f32[1024,128]{1,0:T(8,128)} %get-tuple-element.128.refs_1_, ...), custom_call_target="tpu_custom_call" | custom-call | flops 25165824 | bytes 2097152 | tf_op jit(solution)/shard_map/late/pallas_call | solution.py:261
Async XLA Ops:
  34.9 21.5 %copy-start.36 = (f32[1544,128]{1,0:T(8,128)}, f32[1544,128]{1,0:T(8,128)S(1)}, u32[]{:S(2)}) copy-start(f32[1544,128]{1,0:T(8,128)S(1)} %get-tuple-element.43.refs_0_.refs_4_) | copy-start | bytes 2371588 | tf_op jit(solution)/shard_map/cond
  34.9 15.0 %collective-permute-start = (f32[1032,128]{1,0:T(8,128)}, f32[1032,128]{1,0:T(8,128)S(1)}, u32[]{:S(2)}, u32[]{:S(2)}) collective-permute-start(f32[1032,128]{1,0:T(8,128)} %get-tuple-element.41.refs_0_), channel_id=1, source_target_pairs={{0,1},{1,2},{4,5},{5,6},{8,9},{9,10},{12,13},{13,14},{16,17},{17,1... | collective-permute-start | bytes 1585160 | tf_op jit(solution)/shard_map/cond/branch_0_fun/ppermute | solution.py:393
  38.1 18.2 %collective-permute-start.3 = (f32[1544,128]{1,0:T(8,128)S(1)}, f32[1544,128]{1,0:T(8,128)S(1)}, u32[]{:S(2)}, u32[]{:S(2)}) collective-permute-start(f32[1544,128]{1,0:T(8,128)S(1)} %get-tuple-element.43.refs_0_.refs_4_), channel_id=1, source_target_pairs={{0,8},{4,12},{8,0},{12,4},{16,24},{20,28},{24,16},{28,20},{1,9},{5... | collective-permute-start | bytes 2371592 | tf_op jit(solution)/shard_map/cond/branch_0_fun/ppermute | solution.py:393
  39.4 17.9 %collective-permute-start.4 = (f32[1544,128]{1,0:T(8,128)S(1)}, f32[1544,128]{1,0:T(8,128)S(1)}, u32[]{:S(2)}, u32[]{:S(2)}) collective-permute-start(f32[1544,128]{1,0:T(8,128)S(1)} %get-tuple-element.43.refs_0_.refs_4_), channel_id=1, source_target_pairs={{0,16},{4,20},{8,24},{12,28},{16,0},{20,4},{24,8},{28,12},{1,17},{... | collective-permute-start | bytes 2371592 | tf_op jit(solution)/shard_map/cond/branch_0_fun/ppermute | solution.py:393
  40.6 20.5 %collective-permute-start.10 = (f32[1024,128]{1,0:T(8,128)}, f32[1024,128]{1,0:T(8,128)S(1)}, u32[]{:S(2)}, u32[]{:S(2)}) collective-permute-start(f32[1024,128]{1,0:T(8,128)} %get-tuple-element.52), channel_id=1, source_target_pairs={{0,1},{1,2},{4,5},{5,6},{8,9},{9,10},{12,13},{13,14},{16,17},{17,1... | collective-permute-start | bytes 1572872 | tf_op jit(solution)/shard_map/cond/branch_0_fun/ppermute | solution.py:393
  49.9 21.7 %collective-permute-start.1 = (f32[1032,128]{1,0:T(8,128)S(1)}, f32[1032,128]{1,0:T(8,128)S(1)}, u32[]{:S(2)}, u32[]{:S(2)}) collective-permute-start(f32[1032,128]{1,0:T(8,128)S(1)} %collective-permute-done.refs_1_), channel_id=1, source_target_pairs={{1,2},{2,3},{5,6},{6,7},{9,10},{10,11},{13,14},{14,15},{17,18},{18... | collective-permute-start | bytes 1585160 | tf_op jit(solution)/shard_map/cond/branch_0_fun/ppermute | solution.py:393
  56.4 27.9 %copy-start.8 = (f32[1544,128]{1,0:T(8,128)}, f32[1544,128]{1,0:T(8,128)S(1)}, u32[]{:S(2)}) copy-start(f32[1544,128]{1,0:T(8,128)S(1)} %collective-permute-done.3.refs_1_.refs_5_) | copy-start | bytes 2371588 | tf_op jit(solution)/shard_map/cond
  57.3 27.0 %copy-start.20 = (f32[1544,128]{1,0:T(8,128)}, f32[1544,128]{1,0:T(8,128)S(1)}, u32[]{:S(2)}) copy-start(f32[1544,128]{1,0:T(8,128)S(1)} %collective-permute-done.4.refs_2_.refs_6_) | copy-start | bytes 2371588 | tf_op jit(solution)/shard_map/cond
  57.3 27.0 %collective-permute-start.5 = (f32[1544,128]{1,0:T(8,128)}, f32[1544,128]{1,0:T(8,128)S(1)}, u32[]{:S(2)}, u32[]{:S(2)}) collective-permute-start(f32[1544,128]{1,0:T(8,128)} %copy-done.36), channel_id=1, source_target_pairs={{0,24},{4,28},{8,16},{12,20},{16,8},{20,12},{24,0},{28,4},{1,25},{... | collective-permute-start | bytes 2371592 | tf_op jit(solution)/shard_map/cond/branch_0_fun/ppermute | solution.py:393
  61.1 21.7 %copy-start.42 = (f32[1024,128]{1,0:T(8,128)}, f32[1024,128]{1,0:T(8,128)S(1)}, u32[]{:S(2)}) copy-start(f32[1024,128]{1,0:T(8,128)S(1)} %collective-permute-done.10) | copy-start | bytes 1572868 | tf_op jit(solution)/shard_map/cond
  61.1 21.7 %collective-permute-start.11 = (f32[1024,128]{1,0:T(8,128)S(1)}, f32[1024,128]{1,0:T(8,128)}, u32[]{:S(2)}, u32[]{:S(2)}) collective-permute-start(f32[1024,128]{1,0:T(8,128)S(1)} %collective-permute-done.10), channel_id=1, source_target_pairs={{1,2},{2,3},{5,6},{6,7},{9,10},{10,11},{13,14},{14,15},{17,18},{18... | collective-permute-start | bytes 1572872 | tf_op jit(solution)/shard_map/cond/branch_0_fun/ppermute | solution.py:393
  71.5 64.3 %collective-permute-start.2 = (f32[1032,128]{1,0:T(8,128)S(1)}, f32[1032,128]{1,0:T(8,128)}, u32[]{:S(2)}, u32[]{:S(2)}) collective-permute-start(f32[1032,128]{1,0:T(8,128)S(1)} %collective-permute-done.1.refs_2_), channel_id=1, source_target_pairs={{2,3},{3,0},{6,7},{7,4},{10,11},{11,8},{14,15},{15,12},{18,19},{19... | collective-permute-start | bytes 1585160 | tf_op jit(solution)/shard_map/cond/branch_0_fun/ppermute | solution.py:393
  82.8 67.7 %collective-permute-start.12 = (f32[1024,128]{1,0:T(8,128)}, f32[1024,128]{1,0:T(8,128)}, u32[]{:S(2)}, u32[]{:S(2)}) collective-permute-start(f32[1024,128]{1,0:T(8,128)} %collective-permute-done.11), channel_id=1, source_target_pairs={{2,3},{3,0},{6,7},{7,4},{10,11},{11,8},{14,15},{15,12},{18,19},{19... | collective-permute-start | bytes 1572872 | tf_op jit(solution)/shard_map/cond/branch_0_fun/ppermute | solution.py:393
  84.3 0.9 copy-start.26
  134.2 4.9 %collective-permute-start.7 = (f32[776,128]{1,0:T(8,128)}, f32[776,128]{1,0:T(8,128)S(1)}, u32[]{:S(2)}, u32[]{:S(2)}) collective-permute-start(f32[776,128]{1,0:T(8,128)} %get-tuple-element.45), channel_id=1, source_target_pairs={{0,4},{4,0},{8,12},{12,8},{16,20},{20,16},{24,28},{28,24},{1,5},{5... | collective-permute-start | bytes 1191944 | tf_op jit(solution)/shard_map/cond/branch_0_fun/ppermute | solution.py:393
  135.9 3.3 %collective-permute-start.9 = (f32[776,128]{1,0:T(8,128)}, f32[776,128]{1,0:T(8,128)S(1)}, u32[]{:S(2)}, u32[]{:S(2)}) collective-permute-start(f32[776,128]{1,0:T(8,128)} %get-tuple-element.48), channel_id=1, source_target_pairs={{0,4},{4,0},{8,12},{12,8},{16,20},{20,16},{24,28},{28,24},{1,5},{5... | collective-permute-start | bytes 1191944 | tf_op jit(solution)/shard_map/cond/branch_0_fun/ppermute | solution.py:393
  135.9 2.6 %collective-permute-start.6 = (f32[768,128]{1,0:T(8,128)}, f32[768,128]{1,0:T(8,128)S(1)}, u32[]{:S(2)}, u32[]{:S(2)}) collective-permute-start(f32[768,128]{1,0:T(8,128)} %get-tuple-element.44), channel_id=1, source_target_pairs={{0,4},{4,0},{8,12},{12,8},{16,20},{20,16},{24,28},{28,24},{1,5},{5... | collective-permute-start | bytes 1179656 | tf_op jit(solution)/shard_map/cond/branch_0_fun/ppermute | solution.py:393
  136.4 2.7 %collective-permute-start.8 = (f32[768,128]{1,0:T(8,128)}, f32[768,128]{1,0:T(8,128)S(1)}, u32[]{:S(2)}, u32[]{:S(2)}) collective-permute-start(f32[768,128]{1,0:T(8,128)} %get-tuple-element.46), channel_id=1, source_target_pairs={{0,4},{4,0},{8,12},{12,8},{16,20},{20,16},{24,28},{28,24},{1,5},{5... | collective-permute-start | bytes 1179656 | tf_op jit(solution)/shard_map/cond/branch_0_fun/ppermute | solution.py:393
  139.1 1.1 copy-start.9
  140.3 1.1 copy-start.21
  141.4 1.1 copy-start.27
